TPU v7x, 32 devices: a whole 2x2x4 slice. The times are simulated.
32 devices in a mesh: dp: 4 (over y, x), blk: 8 (over z, core).
Axes of the slice: x: 2, y: 2, z: 4, core: 2. Of those that a mesh axis runs over, the one named last changes fastest.
Arguments:
- inputs: bfloat16 [8, 2048, 768], P('dp', 'blk'), may hold values from -6 to 6
- cotangent: bfloat16 [8, 2048, 768], P('dp', 'blk'), may hold values from -6 to 6
- lengths: int32 [8, 4], P('dp'), may hold values from 1 to 1920, 2048 in all within a row
- view_counts: int32 [8, 4], P('dp'), may hold values from 1 to 2
- padding: int32 [8, 2048], P('dp'), may hold values 0 or 1
- first_gain: float32 [768], replicated, may hold values from 0.5 to 1.5
- query_weight: bfloat16 [768, 768], replicated, may hold values from -0.4375 to 0.4375
- key_value_weight: bfloat16 [768, 1536], replicated, may hold values from -0.21875 to 0.21875
- output_weight: bfloat16 [768, 768], replicated, may hold values from -1.75 to 1.75
- second_gain: float32 [768], replicated, may hold values from 0.5 to 1.5
- expand_weight: bfloat16 [768, 3072], replicated, may hold values from -0.21875 to 0.21875
- contract_weight: bfloat16 [3072, 768], replicated, may hold values from -0.109375 to 0.109375
Outputs:
- result: bfloat16 [8, 2048, 768], P('dp', 'blk')
- grad_inputs: bfloat16 [8, 2048, 768], P('dp', 'blk')
- grad_first_gain: float32 [768], replicated
- grad_query_weight: float32 [768, 768], replicated
- grad_key_value_weight: float32 [768, 1536], replicated
- grad_output_weight: float32 [768, 768], replicated
- grad_second_gain: float32 [768], replicated
- grad_expand_weight: float32 [768, 3072], replicated
- grad_contract_weight: float32 [3072, 768], replicated
Inputs may be any that keep to these rules, and one draw needn't show every extreme that they name: Each row's 4 item lengths add up to 2048, and its longest item has exactly 1920 tokens.
All inputs are finite; a program needn't handle non-finite values. No bound on the sum of `padding` on one device may be relied on, other than what follows from the above.
Results may differ from a plain program's by a relative error of at most 0.017.
Values may be sent and summed in bfloat16 or wider, within the bound.
A program may use at most 256 MiB of HBM per device.

v0:
```python
from functools import partial

import jax
import jax.numpy as jnp
from jax import lax
from jax.sharding import PartitionSpec as P

HEAD = 64
PATCHES = 64


epsilon = 1e-05
lowest = -1e30


def layer_norm(value, gain):
    mean = jnp.mean(value, -1, keepdims=True)
    centred = value - mean
    spread = jnp.mean(centred * centred, -1, keepdims=True)
    return centred * lax.rsqrt(spread + epsilon) * gain


def token_info(lengths, views, positions):
    ends = jnp.cumsum(lengths)
    starts = ends - lengths
    inside = (positions[:, None] >= starts[None, :]) & (positions[:, None] < ends[None, :])
    number = jnp.arange(lengths.shape[0], dtype=jnp.int32)
    item = jnp.sum(jnp.where(inside, number[None, :], 0), 1)
    first = jnp.sum(jnp.where(inside, starts[None, :], 0), 1)
    span = jnp.sum(jnp.where(inside, views[None, :], 0), 1) * PATCHES
    frame = (positions - first) // span
    return (item, frame)


def visible(query_pos, query_item, query_frame, key_pos, key_item, key_frame, key_pad):
    same = query_item[:, None] == key_item[None, :]
    order = key_frame[None, :] <= query_frame[:, None]
    usable = (key_pad[None, :] == 1) | (query_pos[:, None] == key_pos[None, :])
    return same & order & usable


def in_blocks(update, carry, piece, block_rows):
    count = piece[0].shape[0]

    def advance(number, inner):
        begin = number * block_rows
        part = (
            lax.dynamic_slice_in_dim(piece[0], begin, block_rows),
            lax.dynamic_slice_in_dim(piece[1], begin, block_rows),
        )
        return update(inner, part, begin)

    return lax.fori_loop(0, count // block_rows, advance, carry)


def score_parts(query_heads, grad_heads, total, shift, key_heads, value_heads, mask, scale):
    scores = (
        jnp.einsum("qhd,khd->hqk", query_heads, key_heads, preferred_element_type=jnp.float32)
        * scale
    )
    chance = jnp.where(mask[None], jnp.exp(scores - total[..., None]), 0.0)
    chance_grad = jnp.einsum(
        "qhd,khd->hqk", grad_heads, value_heads, preferred_element_type=jnp.float32
    )
    score_grad = (chance * (chance_grad - shift[..., None])).astype(jnp.bfloat16)
    return (chance, score_grad)


def on_device(
    inputs,
    cotangent,
    lengths,
    view_counts,
    padding,
    first_gain,
    query_weight,
    key_value_weight,
    output_weight,
    second_gain,
    expand_weight,
    contract_weight,
):
    micro_count, row_count, width = inputs.shape
    head_count = width // HEAD
    scale = HEAD ** (-0.5)
    cycle_size = lax.axis_size("blk")
    own_start = lax.axis_index("blk") * row_count
    query_positions = own_start + jnp.arange(row_count, dtype=jnp.int32)
    gelu = partial(jax.nn.gelu, approximate=True)
    grads = tuple(
        (
            jnp.zeros(array.shape, jnp.float32)
            for array in (
                first_gain,
                query_weight,
                key_value_weight,
                output_weight,
                second_gain,
                expand_weight,
                contract_weight,
            )
        )
    )
    outputs = []
    input_grads = []
    for micro in range(micro_count):
        row_lengths = lengths[micro]
        row_views = view_counts[micro]
        row_pad = padding[micro]
        query_item, query_frame = token_info(row_lengths, row_views, query_positions)
        flat = inputs[micro].astype(jnp.float32)
        normed, first_pull = jax.vjp(layer_norm, flat, first_gain)
        normed_low = normed.astype(jnp.bfloat16)
        query = jnp.dot(normed_low, query_weight, preferred_element_type=jnp.float32).astype(
            jnp.bfloat16
        )
        pair = jnp.dot(normed_low, key_value_weight, preferred_element_type=jnp.float32).astype(
            jnp.bfloat16
        )
        keys = pair[:, :width]
        values = pair[:, width:]
        query_heads = query.reshape(row_count, head_count, HEAD)

        def mask_for(start, count):
            key_positions = start + jnp.arange(count, dtype=jnp.int32)
            key_item, key_frame = token_info(row_lengths, row_views, key_positions)
            key_pad = lax.dynamic_slice_in_dim(row_pad, start, count)
            return visible(
                query_positions,
                query_item,
                query_frame,
                key_positions,
                key_item,
                key_frame,
                key_pad,
            )

        def forward_block(carry, piece, start):
            count = piece[0].shape[0]
            mask = mask_for(start, count)

            def forward_work(state):
                peak, denominator, weighted = state
                key_heads = piece[0].reshape(count, head_count, HEAD)
                value_heads = piece[1].reshape(count, head_count, HEAD)
                scores = (
                    jnp.einsum(
                        "qhd,khd->hqk", query_heads, key_heads, preferred_element_type=jnp.float32
                    )
                    * scale
                )
                scores = jnp.where(mask[None], scores, lowest)
                new_peak = jnp.maximum(peak, jnp.max(scores, -1))
                raised = jnp.where(mask[None], jnp.exp(scores - new_peak[..., None]), 0.0)
                shrink = jnp.exp(peak - new_peak)
                denominator = denominator * shrink + jnp.sum(raised, -1)
                weighted = weighted * shrink[..., None] + jnp.einsum(
                    "hqk,khd->hqd",
                    raised.astype(jnp.bfloat16),
                    value_heads,
                    preferred_element_type=jnp.float32,
                )
                return (new_peak, denominator, weighted)

            return lax.cond(jnp.any(mask), forward_work, lambda state: state, carry)

        initial = (
            jnp.full((head_count, row_count), lowest, jnp.float32),
            jnp.zeros((head_count, row_count), jnp.float32),
            jnp.zeros((head_count, row_count, HEAD), jnp.float32),
        )
        peak, denominator, weighted = in_blocks(
            forward_block,
            initial,
            (
                lax.all_gather(keys, "blk", axis=0, tiled=True),
                lax.all_gather(values, "blk", axis=0, tiled=True),
            ),
            row_count,
        )
        attended_heads = weighted / denominator[..., None]
        log_total = peak + jnp.log(denominator)
        attended_low = (
            jnp.transpose(attended_heads, (1, 0, 2)).reshape(row_count, width).astype(jnp.bfloat16)
        )
        mixed = flat + jnp.dot(attended_low, output_weight, preferred_element_type=jnp.float32)
        second, second_pull = jax.vjp(layer_norm, mixed, second_gain)
        second_low = second.astype(jnp.bfloat16)
        hidden = jnp.dot(second_low, expand_weight, preferred_element_type=jnp.float32)
        activated, gelu_pull = jax.vjp(gelu, hidden)
        activated_low = activated.astype(jnp.bfloat16)
        output = mixed + jnp.dot(activated_low, contract_weight, preferred_element_type=jnp.float32)
        outputs.append(output.astype(jnp.bfloat16))
        upstream = cotangent[micro]
        grad_contract = jnp.einsum(
            "rf,rd->fd", activated_low, upstream, preferred_element_type=jnp.float32
        )
        activated_grad = jnp.einsum(
            "rd,fd->rf", upstream, contract_weight, preferred_element_type=jnp.float32
        )
        hidden_grad = gelu_pull(activated_grad)[0].astype(jnp.bfloat16)
        grad_expand = jnp.einsum(
            "rd,rf->df", second_low, hidden_grad, preferred_element_type=jnp.float32
        )
        second_grad = jnp.einsum(
            "rf,df->rd", hidden_grad, expand_weight, preferred_element_type=jnp.float32
        )
        mixed_part, grad_second = second_pull(second_grad)
        mixed_grad = upstream.astype(jnp.float32) + mixed_part
        branch_grad = mixed_grad.astype(jnp.bfloat16)
        grad_output = jnp.einsum(
            "rd,re->de", attended_low, branch_grad, preferred_element_type=jnp.float32
        )
        attended_grad = jnp.einsum(
            "re,de->rd", branch_grad, output_weight, preferred_element_type=jnp.float32
        ).astype(jnp.bfloat16)
        grad_heads = attended_grad.reshape(row_count, head_count, HEAD)
        delta = jnp.sum(
            jnp.transpose(grad_heads, (1, 0, 2)).astype(jnp.float32) * attended_heads, -1
        )

        def backward_block(carry, piece, start):
            count = piece[0].shape[0]
            mask = mask_for(start, count)

            def backward_work(state):
                query_sum, pair_terms = state
                key_heads = piece[0].reshape(count, head_count, HEAD)
                value_heads = piece[1].reshape(count, head_count, HEAD)
                chance, score_grad = score_parts(
                    query_heads, grad_heads, log_total, delta, key_heads, value_heads, mask, scale
                )
                value_term = jnp.einsum(
                    "hqk,qhd->khd",
                    chance.astype(jnp.bfloat16),
                    grad_heads,
                    preferred_element_type=jnp.float32,
                )
                query_sum = (
                    query_sum
                    + jnp.einsum(
                        "hqk,khd->qhd", score_grad, key_heads, preferred_element_type=jnp.float32
                    )
                    * scale
                )
                key_term = (
                    jnp.einsum(
                        "hqk,qhd->khd", score_grad, query_heads, preferred_element_type=jnp.float32
                    )
                    * scale
                )
                term = jnp.concatenate(
                    [key_term.reshape(count, width), value_term.reshape(count, width)], 1
                )
                previous = lax.dynamic_slice_in_dim(pair_terms, start, count)
                pair_terms = lax.dynamic_update_slice_in_dim(pair_terms, previous + term, start, 0)
                return (query_sum, pair_terms)

            return lax.cond(jnp.any(mask), backward_work, lambda state: state, carry)

        start_back = (
            jnp.zeros((row_count, head_count, HEAD), jnp.float32),
            jnp.zeros((row_count * cycle_size, 2 * width), jnp.float32),
        )
        back_state = in_blocks(
            backward_block,
            start_back,
            (
                lax.all_gather(keys, "blk", axis=0, tiled=True),
                lax.all_gather(values, "blk", axis=0, tiled=True),
            ),
            row_count,
        )
        query_sum, pair_terms = back_state
        pair_grad = lax.psum_scatter(
            pair_terms.astype(jnp.bfloat16), "blk", scatter_dimension=0, tiled=True
        )
        query_grad = query_sum.reshape(row_count, width).astype(jnp.bfloat16)
        grad_query = jnp.einsum(
            "rd,re->de", normed_low, query_grad, preferred_element_type=jnp.float32
        )
        grad_pair = jnp.einsum(
            "rd,re->de", normed_low, pair_grad, preferred_element_type=jnp.float32
        )
        normed_grad = jnp.einsum(
            "re,de->rd", query_grad, query_weight, preferred_element_type=jnp.float32
        )
        normed_grad = normed_grad + jnp.einsum(
            "re,de->rd", pair_grad, key_value_weight, preferred_element_type=jnp.float32
        )
        input_part, grad_first = first_pull(normed_grad)
        input_grads.append((mixed_grad + input_part).astype(jnp.bfloat16))
        terms = (
            grad_first,
            grad_query,
            grad_pair,
            grad_output,
            grad_second,
            grad_expand,
            grad_contract,
        )
        grads = tuple((total + term for total, term in zip(grads, terms)))
    summed = lax.psum(
        (grads[0], grads[1], grads[2], grads[3], grads[4], grads[5], grads[6]), ("dp", "blk")
    )
    return (
        jnp.stack(outputs),
        jnp.stack(input_grads),
        summed[0],
        summed[1],
        summed[2],
        summed[3],
        summed[4],
        summed[5],
        summed[6],
    )


def solution(mesh):
    placed = (
        P("dp", "blk", None),
        P("dp", "blk", None),
        P("dp", None),
        P("dp", None),
        P("dp", None),
        P(),
        P(),
        P(),
        P(),
        P(),
        P(),
        P(),
    )
    return jax.shard_map(
        on_device,
        mesh=mesh,
        in_specs=placed,
        out_specs=(P("dp", "blk", None), P("dp", "blk", None), P(), P(), P(), P(), P(), P(), P()),
        check_vma=False,
    )
```

profile of v0, /device:TPU:0, one launch (start us, length us, event | category | flops | bytes accessed | tf_op | source)
XLA Modules:
  0.0 1144.1 jit_solution(13924266885800532183)
XLA Ops:
  27.0 27.3 %all-gather.9.cloned.1.call-done = bf16[2048,768]{1,0:T(8,128)(2,1)} async-done(((bf16[256,768]{1,0:T(8,128)(2,1)}), bf16[2048,768]{1,0:T(8,128)(2,1)}) %all-gather.9.cloned.1.call-update) | async-done | bytes 3145744 | tf_op jit(solution)/shard_map/all_gather | solution.py:176
  54.4 4.8 copy.77
  59.1 34.6 %all-gather.11.cloned.1.call-done = bf16[2048,768]{1,0:T(8,128)(2,1)} async-done(((bf16[256,768]{1,0:T(8,128)(2,1)}), bf16[2048,768]{1,0:T(8,128)(2,1)}) %all-gather.11.cloned.1.call-update) | async-done | bytes 3145744 | tf_op jit(solution)/shard_map/all_gather | solution.py:177
  93.7 4.6 copy.78
  98.3 34.8 %all-gather.5.cloned.1.call-done = bf16[2048,768]{1,0:T(8,128)(2,1)} async-done(((bf16[256,768]{1,0:T(8,128)(2,1)}), bf16[2048,768]{1,0:T(8,128)(2,1)}) %all-gather.5.cloned.1.call-update) | async-done | bytes 3145744 | tf_op jit(solution)/shard_map/all_gather | solution.py:176
  133.1 4.6 copy.74
  138.7 34.4 %while.77 = (s32[]{:T(128)}, f32[12,256]{1,0:T(8,128)S(1)}, f32[12,256]{1,0:T(8,128)S(1)}, f32[12,256,64]{1,2,0:T(8,128)}, s32[256]{0:T(256)S(1)}, /*index=5*/s3...) while((s32[]{:T(128)}, f32[12,256]{1,0:T(8,128)S(1)}, ...), condition=%wide.region_33.34_spmd.clone, body=%wide.region_24.33_spmd.clone.sunk | while | flops 212420608 | bytes 20530132 | solution.py:53
  141.8 4.7 conditional.13
  149.6 4.6 conditional.13
  178.1 4.7 copy.75
  183.8 29.2 %while.76 = (s32[]{:T(128)}, f32[12,256]{1,0:T(8,128)S(1)}, f32[12,256]{1,0:T(8,128)S(1)}, f32[12,256,64]{1,2,0:T(8,128)}, s32[256]{0:T(256)S(1)}, /*index=5*/s3...) while((s32[]{:T(128)}, f32[12,256]{1,0:T(8,128)S(1)}, ...), condition=%wide.region_15.16_spmd.clone, body=%wide.region_6.15_spmd.clone.sunk | while | flops 212420608 | bytes 20530132 | solution.py:53
  193.4 4.6 conditional.12
  242.9 6.2 broadcast.585.clone.1
  249.1 67.8 %while.78 = (s32[]{:T(128)}, f32[256,12,64]{0,2,1:T(8,128)}, f32[2048,1536]{0,1:T(8,128)}, s32[256]{0:T(256)S(1)}, s32[1,4]{1,0:T(1,128)S(1)}, /*index=5*/s32[4,...) while((s32[]{:T(128)}, f32[256,12,64]{0,2,1:T(8,128)}, ...), condition=%wide.region_46.47_spmd.clone, body=%wide.region_39.0_spmd.clone.sunk | while | flops 513028096 | bytes 59991480 | solution.py:53
  254.1 11.8 %conditional.14 = ((f32[256,12,64]{0,2,1:T(8,128)}, f32[2048,1536]{0,1:T(8,128)})) conditional(s32[]{:T(128)} %convert_element_type.440, (f32[256,12,64]{0,2,1:T(8,128)}, f32[2048,1536]{0,1:T(8,128)}) %tuple.312, (pred[256,256]{0,1:T(8,128)(4,1)}, bf16[2048,768]{0,1:T(8,128)(2,1)}, s32[]{:T(128)}, bf16[256,12,64]{0,2,1:T(8,128)(2,1)S(1)}, ...), branch_computations={%region_44.44_spmd, %region_45.45_spmd} | conditional | flops 512557056 | bytes 59904316 | solution.py:259
  271.0 11.8 %conditional.14 = ((f32[256,12,64]{0,2,1:T(8,128)}, f32[2048,1536]{0,1:T(8,128)})) conditional(s32[]{:T(128)} %convert_element_type.440, (f32[256,12,64]{0,2,1:T(8,128)}, f32[2048,1536]{0,1:T(8,128)}) %tuple.312, (pred[256,256]{0,1:T(8,128)(4,1)}, bf16[2048,768]{0,1:T(8,128)(2,1)}, s32[]{:T(128)}, bf16[256,12,64]{0,2,1:T(8,128)(2,1)S(1)}, ...), branch_computations={%region_44.44_spmd, %region_45.45_spmd} | conditional | flops 512557056 | bytes 59904316 | solution.py:259
  316.8 8.2 convert_element_type.240
  334.7 6.2 broadcast.585.clone
  340.9 56.5 %while.79 = (s32[]{:T(128)}, f32[256,12,64]{0,2,1:T(8,128)}, f32[2048,1536]{0,1:T(8,128)}, s32[256]{0:T(256)S(1)}, s32[1,4]{1,0:T(1,128)S(1)}, /*index=5*/s32[4,...) while((s32[]{:T(128)}, f32[256,12,64]{0,2,1:T(8,128)}, ...), condition=%wide.region_60.61_spmd.clone, body=%wide.region_53.60_spmd.clone.sunk | while | flops 513028096 | bytes 58414264 | solution.py:53
  344.6 13.2 %conditional.15 = ((f32[256,12,64]{0,2,1:T(8,128)}, f32[2048,1536]{0,1:T(8,128)})) conditional(s32[]{:T(128)} %convert_element_type.441, (f32[256,12,64]{0,2,1:T(8,128)}, f32[2048,1536]{0,1:T(8,128)}) %tuple.318, (pred[256,256]{0,1:T(8,128)(4,1)}, bf16[2048,768]{0,1:T(8,128)(2,1)}, s32[]{:T(128)}, bf16[256,12,64]{0,2,1:T(8,128)(2,1)S(1)}, ...), branch_computations={%region_58.58_spmd, %region_59.59_spmd} | conditional | flops 512557056 | bytes 58331424 | solution.py:259
  361.6 13.2 %conditional.15 = ((f32[256,12,64]{0,2,1:T(8,128)}, f32[2048,1536]{0,1:T(8,128)})) conditional(s32[]{:T(128)} %convert_element_type.441, (f32[256,12,64]{0,2,1:T(8,128)}, f32[2048,1536]{0,1:T(8,128)}) %tuple.318, (pred[256,256]{0,1:T(8,128)(4,1)}, bf16[2048,768]{0,1:T(8,128)(2,1)}, s32[]{:T(128)}, bf16[256,12,64]{0,2,1:T(8,128)(2,1)S(1)}, ...), branch_computations={%region_58.58_spmd, %region_59.59_spmd} | conditional | flops 512557056 | bytes 58331424 | solution.py:259
  397.4 8.2 convert_element_type.250
  419.0 5.3 convolution_add_fusion.1
  424.3 6.1 convolution_add_fusion
  430.4 84.8 %reduce-scatter.3.cloned.1.call-done = bf16[256,1536]{0,1:T(8,128)(2,1)} async-done(((bf16[2048,1536]{0,1:T(8,128)(2,1)}), bf16[256,1536]{0,1:T(8,128)(2,1)}) %reduce-scatter.3.cloned.1.call-update) | async-done | bytes 786448 | tf_op jit(solution)/shard_map/reduce_scatter | solution.py:275
  519.5 155.5 %reduce-scatter.5.cloned.1.call-done = bf16[256,1536]{0,1:T(8,128)(2,1)} async-done(((bf16[2048,1536]{0,1:T(8,128)(2,1)}), bf16[256,1536]{0,1:T(8,128)(2,1)}) %reduce-scatter.5.cloned.1.call-update) | async-done | bytes 786448 | tf_op jit(solution)/shard_map/reduce_scatter | solution.py:275
  675.0 5.8 convolution_add_fusion.2
  681.4 5.7 fusion.74
  687.2 4.6 fusion.75
  696.8 39.7 %all-reduce = (f32[768]{0:T(1024)}, f32[768]{0:T(1024)}) all-reduce(f32[768]{0:T(1024)S(1)} %add.527, f32[768]{0:T(1024)S(1)} %add.531), channel_id=1, replica_groups=mesh['dp'=4,'blk'=8] {'dp','blk'}, use_global_device_ids=true, to_apply=%region_66.67 | all-reduce | flops 1536 | bytes 12288 | tf_op jit(solution)/shard_map/psum | solution.py:303
  740.4 375.4 %all-reduce.4.cloned.1.call-done = (f32[768,768]{1,0:T(8,128)}, f32[768,1536]{1,0:T(8,128)}, f32[768,768]{1,0:T(8,128)}, f32[768,3072]{1,0:T(8,128)}, f32[3072,768]{1,0:T(8,128)}) async-done(((f32[768,768]{1,0:T(8,128)}, f32[768,1536]{1,0:T(8,128)}, f32[768,768]{1,0:T(8,128)}, f32[768,3072]{1,0:T(8,128)}, f32[3072,768]{1,0:T(8,128)}), (f32[768,768]{1,0:T(8,128)}, f32[768,1536]{1,0:T(8,128)}, ...) | async-done | bytes 28311568 | tf_op jit(solution)/shard_map/psum | solution.py:303
  1124.0 9.3 copy.165
  (690 shorter events, 273.4 us)
Async XLA Ops:
  7.2 47.2 %all-gather.9.cloned.1.call-start = ((), (), s32[]{:S(2)}) async-start(), calls=%async_computation.4 | async-start | bytes 3538944 | tf_op jit(solution)/shard_map/all_gather | solution.py:176
  8.7 7.8 copy-start.90
  8.7 10.3 copy-start.88
  13.2 80.5 %all-gather.11.cloned.1.call-start = ((), (), s32[]{:S(2)}) async-start(), calls=%async_computation.5 | async-start | bytes 3538944 | tf_op jit(solution)/shard_map/all_gather | solution.py:177
  13.9 119.2 %all-gather.5.cloned.1.call-start = ((), (), s32[]{:S(2)}) async-start(), calls=%async_computation.2 | async-start | bytes 3538944 | tf_op jit(solution)/shard_map/all_gather | solution.py:176
  15.8 162.3 %all-gather.7.cloned.1.call-start = ((), (), s32[]{:S(2)}) async-start(), calls=%async_computation.3 | async-start | bytes 3538944 | tf_op jit(solution)/shard_map/all_gather | solution.py:177
  16.4 498.8 %reduce-scatter.3.cloned.1.call-start = ((), (), s32[]{:S(2)}) async-start(), calls=%async_computation.6 | async-start | bytes 7077888 | tf_op jit(solution)/shard_map/reduce_scatter | solution.py:275
  21.6 37.5 %copy-start.83 = (s32[4,1]{0,1:T(1,128)}, s32[4,1]{0,1:T(1,128)S(1)}, u32[]{:S(2)}) copy-start(s32[4,1]{0,1:T(1,128)S(1)} %reduce-window.30) | copy-start | bytes 52
  173.1 9.7 copy-start.49
  173.1 9.7 copy-start.59
  173.1 9.7 copy-start.67
  173.1 9.7 copy-start.69
  173.1 9.7 copy-start.76
  173.1 9.7 copy-start.81
  176.4 6.4 copy-start.94
  214.9 6.4 slice-start.3
  217.0 16.5 %copy-start.19 = (f32[256,768]{1,0:T(8,128)}, f32[256,768]{1,0:T(8,128)S(1)}, u32[]{:S(2)}) copy-start(f32[256,768]{1,0:T(8,128)S(1)} %get-tuple-element.2301) | copy-start | bytes 2359300
  217.0 16.5 %copy-start.99 = (f32[256]{0:T(256)}, f32[256]{0:T(256)S(1)}, u32[]{:S(2)}) copy-start(f32[256]{0:T(256)S(1)} %broadcast_multiply_fusion.2) | copy-start | bytes 3076
  217.3 16.2 %copy-start.107 = (f32[256]{0:T(256)}, f32[256]{0:T(256)S(1)}, u32[]{:S(2)}) copy-start(f32[256]{0:T(256)S(1)} %fusion.141) | copy-start | bytes 3076
  254.1 11.8 %copy-start.80 = (s32[1,4]{1,0:T(1,128)S(1)}, s32[1,4]{1,0:T(1,128)}, u32[]{:S(2)}) copy-start(s32[1,4]{1,0:T(1,128)} %get-tuple-element.3099) | copy-start | bytes 52 | tf_op jit(solution)/shard_map/while
  254.1 11.8 %copy-start.87 = (s32[1,4]{1,0:T(1,128)S(1)}, s32[1,4]{1,0:T(1,128)}, u32[]{:S(2)}) copy-start(s32[1,4]{1,0:T(1,128)} %get-tuple-element.3124) | copy-start | bytes 52 | tf_op jit(solution)/shard_map/while
  271.0 11.8 %copy-start.80 = (s32[1,4]{1,0:T(1,128)S(1)}, s32[1,4]{1,0:T(1,128)}, u32[]{:S(2)}) copy-start(s32[1,4]{1,0:T(1,128)} %get-tuple-element.3099) | copy-start | bytes 52 | tf_op jit(solution)/shard_map/while
  271.0 11.8 %copy-start.87 = (s32[1,4]{1,0:T(1,128)S(1)}, s32[1,4]{1,0:T(1,128)}, u32[]{:S(2)}) copy-start(s32[1,4]{1,0:T(1,128)} %get-tuple-element.3124) | copy-start | bytes 52 | tf_op jit(solution)/shard_map/while
  325.0 7.4 copy-start.50
  325.1 349.9 %reduce-scatter.5.cloned.1.call-start = ((), (), s32[]{:S(2)}) async-start(), calls=%async_computation.7 | async-start | bytes 7077888 | tf_op jit(solution)/shard_map/reduce_scatter | solution.py:275
  405.7 710.1 %all-reduce.4.cloned.1.call-start = ((), (), s32[]{:S(2)}) async-start(), calls=%async_computation.8 | async-start | bytes 56623104 | tf_op jit(solution)/shard_map/psum | solution.py:303
  424.3 90.9 %copy-start.14 = (bf16[2,256,768]{2,1,0:T(8,128)(2,1)S(1)}, bf16[2,256,768]{2,1,0:T(8,128)(2,1)}, u32[]{:S(2)}) copy-start(bf16[2,256,768]{2,1,0:T(8,128)(2,1)} %param.28) | copy-start | bytes 2359300
  694.8 41.7 %copy-start.110 = (f32[256]{0:T(256)S(1)}, f32[256]{0:T(256)}, u32[]{:S(2)}) copy-start(f32[256]{0:T(256)} %copy-done.109) | copy-start | bytes 3076
  694.8 41.7 %copy-start.112 = (f32[256]{0:T(256)S(1)}, f32[256]{0:T(256)}, u32[]{:S(2)}) copy-start(f32[256]{0:T(256)} %copy-done.111) | copy-start | bytes 3076
  1122.6 10.7 slice-start
  1124.0 9.3 slice-start.1
  1124.0 9.3 slice-start.2
  (146 other events, 359.9 us)
Sparse Core Ops, SparseCore 0:
  13.3 41.0 all-gather.8
  56.6 37.0 all-gather.10
  95.9 37.1 all-gather.4
  135.2 37.1 all-gather.6
  325.2 189.9 reduce-scatter.2
  517.3 157.5 reduce-scatter.4
  682.5 433.2 all-reduce.3
where the time goes:
time: 1150 us; the launch traced here: 1140 us
  waiting for transfers between devices  714 us (62%)
  other arithmetic  148 us (13%)
  matrix products  107 us (9%)
  local copies, waits for them, and re-layouts  95.9 us (8%)
  blocking collectives  39.7 us (3%)
  loops' own time  23.6 us (2%)
  between operations  15.7 us (1%)
    psum x1, waiting for transfers between devices, on_device(): lax.psum((grads[0], grads[1], grads[2], grads[3], grads[4], grads[5], gra...  375 us
    reduce_scatter x2, waiting for transfers between devices, on_device(): lax.psum_scatter(pair_terms.astype(jnp.bfloat16), 'blk', scatter_dimensio...  240 us
    all_gather x2, waiting for transfers between devices, on_device(): lax.all_gather(keys, 'blk', axis=0, tiled=True)  62.1 us
    unnamed x219, local copies, waits for them, and re-layouts  46.4 us
    psum x1, blocking collectives, on_device(): lax.psum((grads[0], grads[1], grads[2], grads[3], grads[4], grads[5], gra...  39.7 us
    all_gather x2, waiting for transfers between devices, on_device(): lax.all_gather(values, 'blk', axis=0, tiled=True)  34.6 us
    reduce_or x16, other arithmetic, backward_block(): return lax.cond(jnp.any(mask), backward_work, lambda state: state, carry)  29.2 us
    eq x32, other arithmetic, visible(): usable = (key_pad[None, :] == 1) | (query_pos[:, None] == key_pos[None, :])  24.2 us
  transfers between devices with their start and end apart: 7, of which 6 were waited for; matrix products, arithmetic and copies ran while one was open for 15% of the time, Pallas kernels for 0%

commit v1 on v0

--- a/solution.py
+++ b/solution.py
@@ -3,14 +3,621 @@
 import jax
 import jax.numpy as jnp
 from jax import lax
+from jax.experimental import pallas as pl
+from jax.experimental.pallas import tpu as pltpu
 from jax.sharding import PartitionSpec as P
 
 HEAD = 64
 PATCHES = 64
-
+CODES = 40
+BIG = 1e30
+LANES = 128
+MESH = pl.DeviceIdType.MESH
+bf16 = jnp.bfloat16
+f32 = jnp.float32
 
 epsilon = 1e-05
 lowest = -1e30
+
+
+def dot_nn(a, b):
+    return lax.dot_general(a, b, (((1,), (0,)), ((), ())), preferred_element_type=f32)
+
+
+def dot_nt(a, b):
+    return lax.dot_general(a, b, (((1,), (1,)), ((), ())), preferred_element_type=f32)
+
+
+def dot_tn(a, b):
+    return lax.dot_general(a, b, (((0,), (0,)), ((), ())), preferred_element_type=f32)
+
+
+def chip_order(z, step):
+    code = jnp.where(z == 0, 3210, jnp.where(z == 1, 3201, jnp.where(z == 2, 312, 123)))
+    return lax.rem(code // jnp.where(step == 0, 1, jnp.where(step == 1, 10, jnp.where(step == 2, 100, 1000))), 10)
+
+
+def far_order(z, step):
+    return jnp.where(
+        step == 0,
+        lax.rem(z + 2, 4),
+        jnp.where(step == 1, 3 - z, jnp.where(step == 2, z + 1 - 2 * lax.rem(z, 2), z)),
+    )
+
+
+def features(block, rows, lengths, views, row, padded):
+    lane = lax.broadcasted_iota(jnp.int32, (rows, LANES), 1) - HEAD
+    position = block * rows + lax.broadcasted_iota(jnp.int32, (rows, LANES), 0)
+    code = jnp.zeros((rows, LANES), jnp.int32)
+    base = jnp.zeros((rows, LANES), jnp.int32)
+    start = jnp.int32(0)
+    first = jnp.int32(0)
+    for item in range(lengths.shape[1]):
+        length = lengths[row, item]
+        view = views[row, item]
+        offset = position - start
+        inside = (offset >= 0) & (offset < length)
+        frame = (offset >> 6) * (2 - view) + (offset >> 7) * (view - 1)
+        code = jnp.where(inside, first + frame, code)
+        base = jnp.where(inside, first, base)
+        first = first + ((length + 63) >> 6) * (2 - view) + ((length + 127) >> 7) * (view - 1)
+        start = start + length
+    coded = (lane >= 0) & (lane < CODES)
+    key = jnp.where(coded & (lane == code), 1.0, 0.0)
+    key = jnp.where((lane > CODES) & (lane < CODES + 4), 1.0, key)
+    key = jnp.where(lane == CODES, padded, key)
+    hidden = (coded & ((lane < base) | (lane > code))) | (lane == CODES)
+    query = jnp.where(hidden, -BIG, 0.0)
+    return key, query
+
+
+def three_parts(value):
+    high = value.astype(bf16).astype(f32)
+    rest = value - high
+    middle = rest.astype(bf16).astype(f32)
+    low = (rest - middle).astype(bf16).astype(f32)
+    return high, middle, low
+
+
+def spread(value, first, lane):
+    high, middle, low = three_parts(value)
+    return jnp.where(
+        lane == first, high, jnp.where(lane == first + 1, middle, jnp.where(lane == first + 2, low, 0.0))
+    )
+
+
+def pack_heads(heads):
+    half = heads[2].shape[0] // 2
+    wide = jnp.concatenate([heads[0], heads[1]], 1)
+    narrow = jnp.concatenate([heads[2][:half], heads[2][half:]], 1)
+    return wide, narrow
+
+
+def greet_line(dp, me, count):
+    barrier = pltpu.get_barrier_semaphore()
+    for step in range(1, count):
+        pl.semaphore_signal(
+            barrier, inc=1, device_id=(dp, lax.rem(me + step, count)), device_id_type=MESH
+        )
+    pl.semaphore_wait(barrier, count - 1)
+
+
+def forward_kernel(
+    lengths, views, x_ref, gain_ref, pad_ref, wq_ref, wkv_ref,
+    normed, qa, ka, va, o_ref, received,
+    weight, stage, scores, tail, peak, acc, outgoing,
+    sib_send, sib_recv, line_send, line_recv, out_send, out_recv,
+):
+    rows, width = x_ref.shape[1], x_ref.shape[2]
+    blocks = normed.shape[0]
+    heads = qa.shape[0]
+    dp = lax.axis_index("dp")
+    me = lax.axis_index("blk")
+    z = me // 2
+    core = lax.rem(me, 2)
+    sibling = me + 1 - 2 * core
+    lane = lax.broadcasted_iota(jnp.int32, (rows, LANES), 1)
+
+    greet_line(dp, me, blocks)
+
+    def norm(value):
+        value = value.astype(f32)
+        mean = jnp.mean(value, -1, keepdims=True)
+        centred = value - mean
+        var = jnp.mean(centred * centred, -1, keepdims=True)
+        return (centred * lax.rsqrt(var + epsilon) * gain_ref[...]).astype(bf16)
+
+    normed[me] = norm(x_ref[core])
+
+    def line_copy(block, up):
+        return pltpu.make_async_remote_copy(
+            src_ref=normed.at[block],
+            dst_ref=normed.at[block],
+            send_sem=line_send.at[block, up],
+            recv_sem=line_recv.at[block],
+            device_id=(dp, me + (2 if up else -2)),
+            device_id_type=MESH,
+        )
+
+    @pl.when(z < 3)
+    def _():
+        line_copy(me, 1).start()
+
+    @pl.when(z > 0)
+    def _():
+        line_copy(me, 0).start()
+
+    stage[...] = norm(x_ref[1 - core])
+    sib_copy = pltpu.make_async_remote_copy(
+        src_ref=stage,
+        dst_ref=normed.at[me],
+        send_sem=sib_send,
+        recv_sem=sib_recv,
+        device_id=(dp, sibling),
+        device_id_type=MESH,
+    )
+    sib_copy.start()
+
+    gap = jnp.zeros((width, LANES - HEAD), bf16)
+    for chip in range(blocks // 2):
+
+        @pl.when(z == chip)
+        def _():
+            for head in range(heads):
+                at = (chip * heads + head) * HEAD
+                for kind, piece in enumerate(
+                    (
+                        wq_ref[:, at : at + HEAD],
+                        wkv_ref[:, at : at + HEAD],
+                        wkv_ref[:, width + at : width + at + HEAD],
+                    )
+                ):
+                    column = (head * 3 + kind) * LANES
+                    weight[:, column : column + LANES] = jnp.concatenate([piece, gap], 1)
+
+    ones = jnp.where((lane >= HEAD) & (lane < HEAD + 3), -1.0, 0.0)
+
+    @pl.loop(0, blocks)
+    def _(step):
+        chip = chip_order(z, step // 2)
+        block = 2 * chip + lax.rem(core + step, 2)
+
+        @pl.when(step == 1)
+        def _():
+            pltpu.make_async_remote_copy(
+                src_ref=stage,
+                dst_ref=normed.at[sibling],
+                send_sem=sib_send,
+                recv_sem=sib_recv,
+                device_id=(dp, sibling),
+                device_id_type=MESH,
+            ).wait_recv()
+
+        @pl.when(step > 1)
+        def _():
+            pltpu.make_async_remote_copy(
+                src_ref=normed.at[block],
+                dst_ref=normed.at[block],
+                send_sem=line_send.at[block, 0],
+                recv_sem=line_recv.at[block],
+                device_id=(dp, sibling),
+                device_id_type=MESH,
+            ).wait_recv()
+
+        @pl.when((step > 0) & (chip <= z) & (z < 3))
+        def _():
+            line_copy(block, 1).start()
+
+        @pl.when((step > 0) & (chip >= z) & (z > 0))
+        def _():
+            line_copy(block, 0).start()
+
+        pad_row = 1.0 - pad_ref[core, pl.ds(block, 1), :].astype(f32)
+        padded = jnp.transpose(jnp.broadcast_to(pad_row, (LANES, rows)))
+        key, query = features(block, rows, lengths, views, core, padded)
+        out = dot_nn(normed[block], weight[...]).astype(bf16).astype(f32)
+        here = pl.ds(pl.multiple_of(block * rows, rows), rows)
+        for head in range(heads):
+            at = head * 3 * LANES
+            qa[head, here, :] = (out[:, at : at + LANES] * (HEAD**-0.5) + query).astype(bf16)
+            ka[head, here, :] = (out[:, at + LANES : at + 2 * LANES] + key).astype(bf16)
+            va[head, here, :] = (out[:, at + 2 * LANES : at + 3 * LANES] + ones).astype(bf16)
+
+    eye = lax.broadcasted_iota(jnp.int32, (rows, rows), 0) == lax.broadcasted_iota(
+        jnp.int32, (rows, rows), 1
+    )
+    half = LANES
+
+    def out_copy(block):
+        return pltpu.make_async_remote_copy(
+            src_ref=outgoing.at[block],
+            dst_ref=received.at[me],
+            send_sem=out_send.at[block],
+            recv_sem=out_recv.at[me],
+            device_id=(dp, block),
+            device_id_type=MESH,
+        )
+
+    @pl.loop(0, blocks)
+    def _(step):
+        block = 2 * far_order(z, step // 2) + lax.rem(core + step, 2)
+        here = pl.ds(pl.multiple_of(block * rows, rows), rows)
+        last = block == blocks - 1
+        beyond = jnp.where(last, blocks * rows - half, (block + 1) * rows)
+        beyond = pl.ds(pl.multiple_of(beyond, half), half)
+        shut = jnp.where(last, -BIG, 0.0)
+        for head in range(heads):
+            query = qa[head, here, :]
+            s = dot_nt(query, ka[head, here, :])
+            plain = dot_nt(query[:, :HEAD], ka[head, here, :HEAD])
+            s = jnp.where(eye, plain, s)
+            t = dot_nt(query, ka[head, beyond, :]) + shut
+            scores[block, head] = s
+            tail[head] = t
+            peak[head] = jnp.maximum(jnp.maximum(s[:, :LANES], s[:, LANES:]), t)
+
+        @pl.loop(0, block)
+        def _(other):
+            there = pl.ds(pl.multiple_of(other * rows, rows), rows)
+            for head in range(heads):
+                s = dot_nt(qa[head, here, :], ka[head, there, :])
+                scores[other, head] = s
+                peak[head] = jnp.maximum(peak[head], jnp.maximum(s[:, :LANES], s[:, LANES:]))
+
+        for head in range(heads):
+            top = jnp.max(peak[head], -1, keepdims=True)
+            peak[head] = jnp.broadcast_to(top, (rows, LANES))
+            p = jnp.exp(tail[head] - top).astype(bf16)
+            acc[head] = dot_nn(p, va[head, beyond, :])
+
+        @pl.loop(0, block + 1)
+        def _(other):
+            there = pl.ds(pl.multiple_of(other * rows, rows), rows)
+            for head in range(heads):
+                top = peak[head]
+                s = scores[other, head]
+                p = jnp.concatenate(
+                    [jnp.exp(s[:, :LANES] - top), jnp.exp(s[:, LANES:] - top)], 1
+                ).astype(bf16)
+                acc[head] += dot_nn(p, va[head, there, :])
+
+        results = []
+        for head in range(heads):
+            total = acc[head]
+            mass = -total[:, HEAD : HEAD + 1]
+            out = total / mass
+            o_ref[head, here, :] = out
+            results.append(out[:, :HEAD].astype(bf16))
+            log_total = peak[head] + jnp.log(mass)
+            qa[head, here, :] = (
+                qa[head, here, :].astype(f32) - spread(log_total, HEAD + CODES + 1, lane)
+            ).astype(bf16)
+        wide, narrow = pack_heads(results)
+
+        @pl.when(block == me)
+        def _():
+            received[me, :rows, :] = wide
+            received[me, rows:, :] = narrow
+
+        @pl.when(block != me)
+        def _():
+            outgoing[block, :rows, :] = wide
+            outgoing[block, rows:, :] = narrow
+            out_copy(block).start()
+
+    sib_copy.wait_send()
+
+    @pl.loop(0, blocks)
+    def _(block):
+        @pl.when((block // 2 <= z) & (z < 3))
+        def _():
+            line_copy(block, 1).wait_send()
+
+        @pl.when((block // 2 >= z) & (z > 0))
+        def _():
+            line_copy(block, 0).wait_send()
+
+        @pl.when(block != me)
+        def _():
+            out_copy(block).wait_send()
+            pltpu.make_async_remote_copy(
+                src_ref=outgoing.at[block],
+                dst_ref=received.at[block],
+                send_sem=out_send.at[block],
+                recv_sem=out_recv.at[block],
+                device_id=(dp, block),
+                device_id_type=MESH,
+            ).wait_recv()
+
+
+def backward_kernel(
+    grad_ref, normed, qa, ka, va, o_ref,
+    got_query, got_pair, grad_weight,
+    outgoing, received, doa, dq, dk, dv, mine, send_query, send_pair,
+    out_send, out_recv, query_send, query_recv, pair_send, pair_recv,
+):
+    rows, width = grad_ref.shape[1], grad_ref.shape[2]
+    blocks = normed.shape[0]
+    heads = qa.shape[0]
+    dp = lax.axis_index("dp")
+    me = lax.axis_index("blk")
+    z = me // 2
+    core = lax.rem(me, 2)
+    lane = lax.broadcasted_iota(jnp.int32, (rows, LANES), 1)
+    greet_line(dp, me, blocks)
+
+    def send(kind, block):
+        src, dst, send_sem, recv_sem = {
+            "grad": (outgoing, received, out_send, out_recv),
+            "query": (send_query, got_query, query_send, query_recv),
+            "pair": (send_pair, got_pair, pair_send, pair_recv),
+        }[kind]
+        return pltpu.make_async_remote_copy(
+            src_ref=src.at[block],
+            dst_ref=dst.at[me],
+            send_sem=send_sem.at[block],
+            recv_sem=recv_sem.at[me],
+            device_id=(dp, block),
+            device_id_type=MESH,
+        )
+
+    def arrive(kind, block):
+        src, dst, send_sem, recv_sem = {
+            "grad": (outgoing, received, out_send, out_recv),
+            "query": (send_query, got_query, query_send, query_recv),
+            "pair": (send_pair, got_pair, pair_send, pair_recv),
+        }[kind]
+        return pltpu.make_async_remote_copy(
+            src_ref=src.at[block],
+            dst_ref=dst.at[block],
+            send_sem=send_sem.at[block],
+            recv_sem=recv_sem.at[block],
+            device_id=(dp, block),
+            device_id_type=MESH,
+        )
+
+    for chip in range(blocks // 2):
+        for row in range(2):
+            at = chip * heads * HEAD
+            wide, narrow = pack_heads(
+                [grad_ref[row, :, at + h * HEAD : at + (h + 1) * HEAD] for h in range(heads)]
+            )
+            outgoing[2 * chip + row, :rows, :] = wide
+            outgoing[2 * chip + row, rows:, :] = narrow
+
+    for step in range(4):
+        for row in range(2):
+            block = 2 * far_order(z, jnp.int32(step)) + row
+
+            @pl.when(block != me)
+            def _():
+                send("grad", block).start()
+
+    received[me] = outgoing[me]
+
+    @pl.loop(0, blocks)
+    def _(step):
+        block = 2 * chip_order(z, step // 2) + lax.rem(core + step, 2)
+
+        @pl.when(block != me)
+        def _():
+            arrive("grad", block).wait_recv()
+
+        here = pl.ds(pl.multiple_of(block * rows, rows), rows)
+        wide = received[block, :rows, :].astype(f32)
+        narrow = received[block, rows:, :].astype(f32)
+        pieces = [
+            wide[:, :HEAD],
+            wide[:, HEAD:],
+            jnp.concatenate([narrow[:, :HEAD], narrow[:, HEAD:]], 0),
+        ]
+        gap = jnp.zeros((rows, LANES - HEAD), f32)
+        for head in range(heads):
+            value = jnp.concatenate([pieces[head], gap], 1)
+            delta = jnp.sum(value * o_ref[head, here, :], -1, keepdims=True)
+            doa[head, here, :] = (value + spread(delta, HEAD, lane)).astype(bf16)
+            dq[head, here, :] = jnp.zeros((rows, LANES), f32)
+
+    eye = lax.broadcasted_iota(jnp.int32, (rows, rows), 0) == lax.broadcasted_iota(
+        jnp.int32, (rows, rows), 1
+    )
+    bare = (lane < HEAD) | (lane > HEAD + CODES)
+    half = LANES
+
+    def pull(head, keys, queries, diagonal, first):
+        k = ka[head, keys, :]
+        q = qa[head, queries, :]
+        g = doa[head, queries, :]
+        s = dot_nt(k, q)
+        if diagonal:
+            s = jnp.where(eye, dot_nt(jnp.where(bare, k, 0.0).astype(bf16), q), s)
+        p = jnp.exp(s)
+        ds = (p * dot_nt(va[head, keys, :], g)).astype(bf16)
+        p = p.astype(bf16)
+        count = k.shape[0]
+        if first:
+            dv[head] = dot_nn(p, g)
+            dk[head] = dot_nn(ds, q)
+        else:
+            dv[head, :count] += dot_nn(p, g)
+            dk[head, :count] += dot_nn(ds, q)
+        dq[head, queries, :] += dot_tn(ds, k)
+
+    @pl.loop(0, blocks)
+    def _(step):
+        block = jnp.where(lax.rem(step, 2) == 0, step // 2, blocks - 1 - step // 2)
+        here = pl.ds(pl.multiple_of(block * rows, rows), rows)
+        for head in range(heads):
+            pull(head, here, here, True, True)
+
+        @pl.loop(block + 1, blocks)
+        def _(other):
+            there = pl.ds(pl.multiple_of(other * rows, rows), rows)
+            for head in range(heads):
+                pull(head, here, there, False, False)
+
+        @pl.when(block > 0)
+        def _():
+            keys = pl.ds(pl.multiple_of(block * rows, rows), half)
+            queries = pl.ds(pl.multiple_of(block * rows - half, half), half)
+            for head in range(heads):
+                pull(head, keys, queries, False, False)
+
+        for head in range(heads):
+            mine[head, here, :] = jnp.concatenate(
+                [dk[head][:, :HEAD], dv[head][:, :HEAD]], 1
+            ).astype(bf16)
+
+        @pl.when(block == me)
+        def _():
+            for head in range(heads):
+                got_pair[me, head * rows : (head + 1) * rows, :] = mine[head, here, :]
+
+        @pl.when(block != me)
+        def _():
+            for head in range(heads):
+                send_pair[block, head * rows : (head + 1) * rows, :] = mine[head, here, :]
+            send("pair", block).start()
+
+    @pl.loop(0, blocks)
+    def _(step):
+        block = 2 * far_order(z, step // 2) + lax.rem(core + step, 2)
+        here = pl.ds(pl.multiple_of(block * rows, rows), rows)
+        parts = [(dq[h, here, :][:, :HEAD] * (HEAD**-0.5)).astype(bf16) for h in range(heads)]
+        wide, narrow = pack_heads(parts)
+        mine[heads, here, :] = wide
+        mine[heads + 1, here, :] = jnp.concatenate(
+            [parts[2], jnp.zeros((rows, LANES - HEAD), bf16)], 1
+        )
+
+        @pl.when(block == me)
+        def _():
+            got_query[me, :rows, :] = wide
+            got_query[me, rows:, :] = narrow
+
+        @pl.when(block != me)
+        def _():
+            send_query[block, :rows, :] = wide
+            send_query[block, rows:, :] = narrow
+            send("query", block).start()
+
+    for tile in range(heads + 2):
+        grad_weight[:, tile * LANES : (tile + 1) * LANES] = jnp.zeros((width, LANES), f32)
+
+    @pl.loop(0, blocks)
+    def _(block):
+        here = pl.ds(pl.multiple_of(block * rows, rows), rows)
+        right = jnp.concatenate([mine[tile, here, :] for tile in range(heads + 2)], 1)
+        grad_weight[...] += dot_tn(normed[block], right)
+
+    @pl.loop(0, blocks)
+    def _(block):
+        @pl.when(block != me)
+        def _():
+            send("grad", block).wait_send()
+            send("query", block).wait_send()
+            send("pair", block).wait_send()
+            arrive("query", block).wait_recv()
+            arrive("pair", block).wait_recv()
+
+
+VMEM = pl.BlockSpec(memory_space=pltpu.VMEM)
+SMEM = pl.BlockSpec(memory_space=pltpu.SMEM)
+
+
+def attention_forward(inputs, gain, lengths, views, padding, query_weight, pair_weight, blocks):
+    micro, rows, width = inputs.shape
+    total = rows * blocks
+    heads = width // HEAD // (blocks // micro)
+    packed = rows * heads // 2
+    shape = jax.ShapeDtypeStruct
+    dma = pltpu.SemaphoreType.DMA
+    return pl.pallas_call(
+        forward_kernel,
+        out_shape=(
+            shape((blocks, rows, width), bf16),
+            shape((heads, total, LANES), bf16),
+            shape((heads, total, LANES), bf16),
+            shape((heads, total, LANES), bf16),
+            shape((heads, total, LANES), f32),
+            shape((blocks, packed, LANES), bf16),
+        ),
+        in_specs=[SMEM, SMEM] + [VMEM] * 5,
+        out_specs=(VMEM,) * 6,
+        scratch_shapes=[
+            pltpu.VMEM((width, heads * 3 * LANES), bf16),
+            pltpu.VMEM((rows, width), bf16),
+            pltpu.VMEM((blocks, heads, rows, rows), f32),
+            pltpu.VMEM((heads, rows, LANES), f32),
+            pltpu.VMEM((heads, rows, LANES), f32),
+            pltpu.VMEM((heads, rows, LANES), f32),
+            pltpu.VMEM((blocks, packed, LANES), bf16),
+            dma,
+            dma,
+            dma((blocks, 2)),
+            dma((blocks,)),
+            dma((blocks,)),
+            dma((blocks,)),
+        ],
+        compiler_params=pltpu.CompilerParams(
+            collective_id=0, has_side_effects=True, vmem_limit_bytes=60 << 20
+        ),
+        name="attention_forward",
+    )(lengths, views, inputs, gain.reshape(1, width), padding.reshape(micro, blocks, rows), query_weight, pair_weight)
+
+
+def attention_backward(grad, normed, qa, ka, va, out):
+    micro, rows, width = grad.shape
+    blocks = normed.shape[0]
+    heads, total, _ = qa.shape
+    packed = rows * heads // 2
+    shape = jax.ShapeDtypeStruct
+    dma = pltpu.SemaphoreType.DMA
+    return pl.pallas_call(
+        backward_kernel,
+        out_shape=(
+            shape((blocks, packed, LANES), bf16),
+            shape((blocks, heads * rows, LANES), bf16),
+            shape((width, (heads + 2) * LANES), f32),
+        ),
+        in_specs=[VMEM] * 6,
+        out_specs=(VMEM,) * 3,
+        scratch_shapes=[
+            pltpu.VMEM((blocks, packed, LANES), bf16),
+            pltpu.VMEM((blocks, packed, LANES), bf16),
+            pltpu.VMEM((heads, total, LANES), bf16),
+            pltpu.VMEM((heads, total, LANES), f32),
+            pltpu.VMEM((heads, rows, LANES), f32),
+            pltpu.VMEM((heads, rows, LANES), f32),
+            pltpu.VMEM((heads + 2, total, LANES), bf16),
+            pltpu.VMEM((blocks, packed, LANES), bf16),
+            pltpu.VMEM((blocks, heads * rows, LANES), bf16),
+            dma((blocks,)),
+            dma((blocks,)),
+            dma((blocks,)),
+            dma((blocks,)),
+            dma((blocks,)),
+            dma((blocks,)),
+        ],
+        compiler_params=pltpu.CompilerParams(
+            collective_id=1, has_side_effects=True, vmem_limit_bytes=60 << 20
+        ),
+        name="attention_backward",
+    )(grad, normed, qa, ka, va, out)
+
+
+def unpack_heads(packed, rows):
+    wide = packed[..., :rows, :]
+    narrow = packed[..., rows:, :]
+    third = jnp.concatenate([narrow[..., :HEAD], narrow[..., HEAD:]], -2)
+    return jnp.concatenate([wide, third], -1)
+
+
+def by_token(received, rows):
+    parts = unpack_heads(received, rows)
+    chips = parts.shape[0] // 2
+    parts = parts.reshape(chips, 2, rows, -1)
+    return jnp.transpose(parts, (1, 2, 0, 3)).reshape(2 * rows, -1)
 
 
 def layer_norm(value, gain):
@@ -316,6 +923,66 @@
     )
 
 
+def fast_on_device(
+    inputs, cotangent, lengths, view_counts, padding, first_gain, query_weight, key_value_weight,
+    output_weight, second_gain, expand_weight, contract_weight,
+):
+    micro, rows, width = inputs.shape
+    blocks = lax.axis_size("blk")
+    normed_all, qa, ka, va, out, received = attention_forward(
+        inputs, first_gain, lengths, view_counts, padding, query_weight, key_value_weight, blocks
+    )
+    gelu = partial(jax.nn.gelu, approximate=True)
+    flat = inputs.reshape(micro * rows, width).astype(f32)
+    upstream = cotangent.reshape(micro * rows, width)
+    _, first_pull = jax.vjp(layer_norm, flat, first_gain)
+    attended = by_token(received, rows)
+    mixed = flat + jnp.dot(attended, output_weight, preferred_element_type=f32)
+    second, second_pull = jax.vjp(layer_norm, mixed, second_gain)
+    second = second.astype(bf16)
+    hidden = jnp.dot(second, expand_weight, preferred_element_type=f32)
+    activated, gelu_pull = jax.vjp(gelu, hidden)
+    activated = activated.astype(bf16)
+    result = (mixed + jnp.dot(activated, contract_weight, preferred_element_type=f32)).astype(bf16)
+    hidden_grad = gelu_pull(dot_nt(upstream, contract_weight))[0].astype(bf16)
+    second_grad = dot_nt(hidden_grad, expand_weight)
+    mixed_part, grad_second = second_pull(second_grad)
+    mixed_grad = upstream.astype(f32) + mixed_part
+    branch_grad = mixed_grad.astype(bf16)
+    attended_grad = dot_nt(branch_grad, output_weight).astype(bf16)
+    grad_contract = dot_tn(activated, upstream)
+    grad_expand = dot_tn(second, hidden_grad)
+    grad_output = dot_tn(attended, branch_grad)
+    got_query, got_pair, unit_grad = attention_backward(
+        attended_grad.reshape(micro, rows, width), normed_all, qa, ka, va, out
+    )
+    heads = qa.shape[0]
+    chips = blocks // 2
+    query_grad = by_token(got_query, rows)
+    pair_grad = got_pair.reshape(chips, 2, heads, rows, 2, HEAD)
+    pair_grad = jnp.transpose(pair_grad, (1, 3, 4, 0, 2, 5)).reshape(micro * rows, 2 * width)
+    normed_grad = dot_nt(query_grad, query_weight) + dot_nt(pair_grad, key_value_weight)
+    input_part, grad_first = first_pull(normed_grad)
+    input_grad = (mixed_grad + input_part).astype(bf16)
+    z = lax.axis_index("blk") // 2
+    pair_part = unit_grad[:, : heads * LANES].reshape(width, heads, 2, HEAD)
+    pair_part = jnp.transpose(pair_part, (0, 2, 1, 3)).reshape(width, 2, heads * HEAD)
+    query_part = unit_grad[:, heads * LANES : heads * LANES + heads * HEAD]
+    grad_pair = lax.dynamic_update_slice(
+        jnp.zeros((width, 2, width), f32), pair_part, (0, 0, z * heads * HEAD)
+    ).reshape(width, 2 * width)
+    grad_query = lax.dynamic_update_slice(
+        jnp.zeros((width, width), f32), query_part, (0, z * heads * HEAD)
+    )
+    wide = [g.astype(bf16) for g in (grad_query, grad_pair, grad_output, grad_expand, grad_contract)]
+    wide = [g.astype(f32) for g in lax.psum(tuple(wide), ("dp", "blk"))]
+    gains = lax.psum((grad_first, grad_second), ("dp", "blk"))
+    return (
+        result.reshape(micro, rows, width), input_grad.reshape(micro, rows, width),
+        gains[0], wide[0], wide[1], wide[2], gains[1], wide[3], wide[4],
+    )
+
+
 def solution(mesh):
     placed = (
         P("dp", "blk", None),
@@ -323,18 +990,28 @@
         P("dp", None),
         P("dp", None),
         P("dp", None),
-        P(),
-        P(),
-        P(),
-        P(),
-        P(),
-        P(),
-        P(),
-    )
-    return jax.shard_map(
-        on_device,
-        mesh=mesh,
-        in_specs=placed,
-        out_specs=(P("dp", "blk", None), P("dp", "blk", None), P(), P(), P(), P(), P(), P(), P()),
-        check_vma=False,
-    )
+    ) + (P(),) * 7
+
+    def program(*arrays):
+        inputs, lengths = arrays[0], arrays[2]
+        dp, blk = mesh.shape["dp"], mesh.shape["blk"]
+        rows, total, width = inputs.shape
+        items = lengths.shape[1]
+        chips = blk // 2
+        fits = (
+            (dp, blk) == (4, 8)
+            and rows == 2 * dp
+            and total % (blk * 2 * LANES) == 0
+            and width % (LANES * HEAD // 64) == 0
+            and width // HEAD == 3 * chips
+            and total // PATCHES + items <= CODES
+        )
+        return jax.shard_map(
+            fast_on_device if fits else on_device,
+            mesh=mesh,
+            in_specs=placed,
+            out_specs=(P("dp", "blk", None), P("dp", "blk", None)) + (P(),) * 7,
+            check_vma=False,
+        )(*arrays)
+
+    return program

time: 1150 us -> 680 us (0.59)
  waiting for transfers between devices: 714 us -> 179 us
  Pallas kernels: 0 us -> 190 us
  other arithmetic: 148 us -> 23.3 us
  blocking collectives: 39.7 us -> 150 us
  matrix products: 107 us -> 45.4 us
  local copies, waits for them, and re-layouts: 95.9 us -> 70.3 us
  loops' own time: 23.6 us -> 0 us
    reduce_scatter x2 -> x0, waiting for transfers between devices: 240 us -> none  [on_device(): lax.psum_scatter(pair_terms.astype(jnp.bfloat16), 'blk', scatter_dimensio...]
    psum x1, waiting for transfers between devices: 375 us -> 179 us  [fast_on_device(): wide = [g.astype(f32) for g in lax.psum(tuple(wide), ('dp', 'blk'))]]
    pallas_call x0 -> x2, Pallas kernels: none -> 190 us  [the longest x1 100 us: attention_forward(): pl.pallas_call(forward_kernel, out_shape=(shape((blocks, rows, width), bf...]
    psum x1, blocking collectives: 39.7 us -> 150 us  [fast_on_device(): gains = lax.psum((grad_first, grad_second), ('dp', 'blk'))]
    all_gather x4 -> x0, waiting for transfers between devices: 96.7 us -> none  [the longest x2 62.1 us: on_device(): lax.all_gather(keys, 'blk', axis=0, tiled=True)]
    dot_general x58 -> x11, matrix products: 107 us -> 45.4 us  [the longest x3 14.9 us: dot_tn(): lax.dot_general(a, b, (((0,), (0,)), ((), ())), preferred_element_type=f32)]
    reduce_or x32 -> x0, other arithmetic: 42.6 us -> none  [the longest x16 29.2 us: backward_block(): return lax.cond(jnp.any(mask), backward_work, lambda state: state, carry)]
    dynamic_update_slice x0 -> x2, local copies, waits for them, and re-layouts: none -> 36.4 us  [the longest x1 32.5 us: fast_on_device(): lax.dynamic_update_slice(jnp.zeros((width, 2, width), f32), pair_part, (0...]
  transfers between devices with their start and end apart: 7 -> 1, of which waited for: 6 -> 1; matrix products, arithmetic and copies ran while one was open for 15% -> 4% of each run, Pallas kernels for 0% -> 0%
where the time goes in v1:
time: 680 us; the launch traced here: 673 us
  Pallas kernels  190 us (28%)
  waiting for transfers between devices  179 us (26%)
  blocking collectives  150 us (22%)
  local copies, waits for them, and re-layouts  70.3 us (10%)
  matrix products  45.4 us (7%)
  other arithmetic  23.3 us (3%)
  between operations  14.8 us (2%)
    psum x1, waiting for transfers between devices, fast_on_device(): wide = [g.astype(f32) for g in lax.psum(tuple(wide), ('dp', 'blk'))]  179 us
    psum x1, blocking collectives, fast_on_device(): gains = lax.psum((grad_first, grad_second), ('dp', 'blk'))  150 us
    pallas_call x1, Pallas kernels, attention_forward(): pl.pallas_call(forward_kernel, out_shape=(shape((blocks, rows, width), bf...  100 us
    pallas_call x1, Pallas kernels, attention_backward(): pl.pallas_call(backward_kernel, out_shape=(shape((blocks, packed, LANES),...  89.6 us
    dynamic_update_slice x1, local copies, waits for them, and re-layouts, fast_on_device(): lax.dynamic_update_slice(jnp.zeros((width, 2, width), f32), pair_part, (0...  32.5 us
    convert_element_type x5, other arithmetic, fast_on_device(): wide = [g.astype(f32) for g in lax.psum(tuple(wide), ('dp', 'blk'))]  17.1 us
    dot_general x3, matrix products, dot_tn(): lax.dot_general(a, b, (((0,), (0,)), ((), ())), preferred_element_type=f32)  14.9 us
    unnamed x53, local copies, waits for them, and re-layouts  13.9 us
  transfers between devices with their start and end apart: 1, of which 1 were waited for; matrix products, arithmetic and copies ran while one was open for 4% of the time, Pallas kernels for 0%

profile of v1, /device:TPU:0, one launch (start us, length us, event | category | flops | bytes accessed | tf_op | source)
XLA Modules:
  0.0 672.9 jit_solution(8460660912161611611)
XLA Ops:
  7.2 1.4 reshape.140.gain_ref
  8.6 1.3 copy.36
  9.9 100.4 %attention_forward.1 = (bf16[8,256,768]{2,1,0:T(8,128)(2,1)}, bf16[3,2048,128]{2,1,0:T(8,128)(2,1)}, bf16[3,2048,128]{2,1,0:T(8,128)(2,1)}, bf16[3,2048,128]{2,1...) custom-call(s32[2,4]{1,0:T(2,128)} %lengths.1, s32[2,4]{1,0:T(2,128)} %views.1, ...), custom_call_target="tpu_custom_call" | custom-call | tf_op jit(solution)/shard_map/attention_forward/pallas_call | solution.py:535
  112.9 1.9 copy.21
  117.4 1.6 copy-done.18
  119.3 2.6 fusion.24
  122.0 8.7 %fusion.6 = (bf16[512,3072]{1,0:T(8,128)(2,1)S(1)}, f32[512,3072]{1,0:T(8,128)}) fusion(f32[512,3072]{1,0:T(8,128)S(1)} %fusion.24, bf16[768,3072]{1,0:T(8,128)(2,1)S(1)} %bitcast.110, f32[512,768]{1,0:T(8,128)S(1)} %get-tuple-element.49, f32[768]{0:T(1024)S(1)} %copy-done.17, f32[512]{0:T(512)S(1)} %fusion.16, f32[512]{0:T(512)S(1)} %broadcast_multiply_fusion.1), kind=kOutput, calls=%fused_computation.8 | convolution fusion | flops 2448949248 | bytes 22027264 | tf_op jit(solution)/shard_map/dot_general | solution.py:943
  130.7 3.4 multiply_reduce_fusion
  134.1 4.8 convolution_convert_fusion.1
  140.7 1.8 convolution_convert_fusion.2
  142.5 1.7 convolution_convert_fusion.3
  144.2 89.6 %attention_backward.1 = (bf16[8,384,128]{2,1,0:T(8,128)(2,1)}, bf16[8,768,128]{2,1,0:T(8,128)(2,1)}, f32[768,640]{1,0:T(8,128)}) custom-call(bf16[2,256,768]{2,1,0:T(8,128)(2,1)} %bitcast.99, bf16[8,256,768]{2,1,0:T(8,128)(2,1)} %get-tuple-element.19.normed, bf16[3,2048,128]{2,1,0:T(8,128)(2,1)} %get-tuple-element.20.qa, ...), custom_call_target="tpu_custom_call" | custom-call | tf_op jit(solution)/shard_map/attention_backward/pallas_call | solution.py:576
  235.0 1.3 slice.37
  236.4 8.3 %convolution_convert_fusion = bf16[3072,768]{1,0:T(8,128)(2,1)} fusion(bf16[512,768]{1,0:T(8,128)(2,1)S(1)} %bitcast.95, f32[512,3072]{1,0:T(8,128)} %get-tuple-element.51), kind=kOutput, calls=%fused_computation.10 | convolution fusion | flops 2432434176 | bytes 11796480 | tf_op jit(solution)/shard_map/dot_general | solution.py:32
  245.6 2.6 broadcast_in_dim.29
  248.3 32.5 %dynamic_update_slice.7 = bf16[768,2,768]{2,1,0:T(2,128)(2,1)} dynamic-update-slice(bf16[768,2,768]{2,1,0:T(2,128)(2,1)} %broadcast_in_dim.29, bf16[768,2,192]{2,1,0:T(2,128)(2,1)S(1)} %copy.27, s32[]{:T(128)} %constant.49.clone.1, s32[]{:T(128)} %constant.49.clone.1, s32[]{:T(128)S(6)} %select_n.10) | dynamic-update-slice | bytes 1179652 | tf_op jit(solution)/shard_map/dynamic_update_slice | solution.py:971
  280.8 3.5 copy.34
  284.4 3.9 dynamic_update_slice.6
  289.9 1.7 copy.23
  291.6 2.1 reshape.149
  293.7 3.5 copy.24
  297.2 1.5 copy.31
  301.4 3.2 fusion.25
  306.6 150.0 %all-reduce = (f32[768]{0:T(1024)}, f32[768]{0:T(1024)}) all-reduce(f32[768]{0:T(1024)S(1)} %get-tuple-element.29, f32[768]{0:T(1024)S(1)} %copy-done.16), channel_id=1, replica_groups=mesh['dp'=4,'blk'=8] {'dp','blk'}, use_global_device_ids=true, to_apply=%region_9.0 | all-reduce | flops 1536 | bytes 12288 | tf_op jit(solution)/shard_map/psum | solution.py:979
  456.6 3.1 add_convert_fusion
  459.7 8.9 %add_convert_fusion.1 = bf16[512,768]{1,0:T(8,128)(2,1)} fusion(f32[512,768]{1,0:T(8,128)S(1)} %copy-done.5, bf16[3072,768]{1,0:T(8,128)(2,1)} %param.23, f32[512,3072]{1,0:T(8,128)} %get-tuple-element.51), kind=kOutput, calls=%fused_computation.30 | convolution fusion | flops 2430861312 | bytes 13369344 | tf_op jit(solution)/shard_map/dot_general | solution.py:946
  468.6 179.1 %all-reduce.4.cloned.1.call-done = (bf16[768,768]{1,0:T(8,128)(2,1)}, bf16[768,1536]{1,0:T(8,128)(2,1)}, bf16[768,768]{1,0:T(8,128)(2,1)}, bf16[768,3072]{1,0:T(8,128)(2,1)}, bf16[3072,768]{1,0:T(8,128)(2,1)}) async-done(((bf16[768,768]{1,0:T(8,128)(2,1)}, bf16[768,1536]{1,0:T(8,128)(2,1)}, bf16[768,768]{1,0:T(8,128)(2,1)}, bf16[768,3072]{1,0:T(8,128)(2,1)}, bf16[3072,768]{1,0:T(8,128)(2,1)}), ...) | async-done | bytes 14155792 | tf_op jit(solution)/shard_map/psum | solution.py:978
  647.8 2.9 convert_element_type.79
  650.7 1.6 convert_element_type.84
  653.2 3.0 convert_element_type.82
  656.3 5.0 convert_element_type.86
  661.3 4.5 convert_element_type.88
  (81 shorter events, 16.4 us)
Async XLA Ops:
  7.2 108.9 %copy-start = (bf16[768,768]{1,0:T(8,128)(2,1)S(1)}, bf16[768,768]{1,0:T(8,128)(2,1)}, u32[]{:S(2)}) copy-start(bf16[768,768]{1,0:T(8,128)(2,1)} %param.20) | copy-start | bytes 3538948
  7.2 640.6 %all-reduce.4.cloned.1.call-start = ((), (), s32[]{:S(2)}) async-start(), calls=%async_computation | async-start | bytes 28311552 | tf_op jit(solution)/shard_map/psum | solution.py:978
  112.8 3.2 copy-start.2
  116.1 2.9 copy-start.18
  117.0 21.9 %copy-start.4 = (f32[512,768]{1,0:T(8,128)}, f32[512,768]{1,0:T(8,128)S(1)}, u32[]{:S(2)}) copy-start(f32[512,768]{1,0:T(8,128)S(1)} %get-tuple-element.49) | copy-start | bytes 4718596
  117.0 2.3 copy-start.9
  117.0 4.9 slice-start.2
  119.3 2.7 copy-start.17
  119.3 2.7 slice-start.3
  139.6 1.2 copy-start.3
  288.3 1.0 copy-start.6
  297.2 1.5 copy-start.13
  300.0 1.4 copy-start.12
  301.4 3.2 copy-start.8
  301.4 3.2 copy-start.15
  305.7 0.8 copy-start.16
  305.7 150.8 %copy-start.10 = (bf16[2,256,768]{2,1,0:T(8,128)(2,1)S(1)}, bf16[2,256,768]{2,1,0:T(8,128)(2,1)}, u32[]{:S(2)}) copy-start(bf16[2,256,768]{2,1,0:T(8,128)(2,1)} %param.13) | copy-start | bytes 2359300
  456.6 3.1 copy-start.5
  647.8 2.9 copy-start.14
  650.7 2.5 copy-start.11
  650.7 5.6 copy-start.7
  653.2 8.1 %slice-start = ((s8[4718592]{0:T(1024)(128)(4,1)}), s8[4194304]{0:T(1024)(128)(4,1)S(1)}, s32[]{:S(2)}) async-start(s8[4718592]{0:T(1024)(128)(4,1)} %bitcast.87), calls=%async_computation.1 | async-start | bytes 8388608
  656.3 5.1 slice-start.1
  661.3 4.5 copy-start.1
Sparse Core Ops, SparseCore 0:
  289.4 358.2 all-reduce.3

commit v2 on v1

--- a/solution.py
+++ b/solution.py
@@ -11,6 +11,16 @@
 PATCHES = 64
 CODES = 40
 BIG = 1e30
+EARLY = 6
+OUT_AT = (0, 3, 6, 9, 12)
+BACK_AT = (0, 3, 6, 9)
+LATE = 13
+GIVE = 4
+PAIR_SLOTS = (10, 14, 18, 21, 23, 24, 22)
+QUERY_SLOTS = (25, 27, 29, 31, 33, 34, 27)
+UNIT_SLOTS = (1, 3, 5, 8, 11, 14, 16)
+OUT = (1, 2, 3, 4, 5)
+BACK = (6, 7, 8, 9)
 LANES = 128
 MESH = pl.DeviceIdType.MESH
 bf16 = jnp.bfloat16
@@ -34,7 +44,18 @@
 
 def chip_order(z, step):
     code = jnp.where(z == 0, 3210, jnp.where(z == 1, 3201, jnp.where(z == 2, 312, 123)))
-    return lax.rem(code // jnp.where(step == 0, 1, jnp.where(step == 1, 10, jnp.where(step == 2, 100, 1000))), 10)
+    return digit(code, step)
+
+
+def digit(code, step):
+    power = jnp.where(step == 0, 1, jnp.where(step == 1, 10, jnp.where(step == 2, 100, 1000)))
+    return lax.rem(code // power, 10)
+
+
+def chip_span(z, step):
+    low = jnp.where(z == 0, 0, jnp.where(z == 1, 1, jnp.where(z == 2, 112, 123)))
+    high = jnp.where(z == 0, 3210, jnp.where(z == 1, 3211, jnp.where(z == 2, 3322, 3333)))
+    return digit(low, step), digit(high, step)
 
 
 def far_order(z, step):
@@ -93,20 +114,51 @@
     return wide, narrow
 
 
-def greet_line(dp, me, count):
+def greet(dp, me, count, others=()):
     barrier = pltpu.get_barrier_semaphore()
     for step in range(1, count):
         pl.semaphore_signal(
             barrier, inc=1, device_id=(dp, lax.rem(me + step, count)), device_id_type=MESH
         )
-    pl.semaphore_wait(barrier, count - 1)
+    for other in others:
+        pl.semaphore_signal(barrier, inc=1, device_id=other, device_id_type=MESH)
+    return lambda: pl.semaphore_wait(barrier, count - 1 + len(others))
+
+
+def heads_of(wide, narrow):
+    return [
+        wide[:, :HEAD],
+        wide[:, HEAD:],
+        jnp.concatenate([narrow[:, :HEAD], narrow[:, HEAD:]], 0),
+    ]
+
+
+def columns_of(received, row, rows, blocks):
+    pieces = []
+    for chip in range(blocks // 2):
+        block = 2 * chip + row
+        pieces += heads_of(received[block, :rows, :], received[block, rows:, :])
+    return jnp.concatenate(pieces, 1)
+
+
+def normal(value):
+    mean = jnp.mean(value, -1, keepdims=True)
+    centred = value - mean
+    scale = lax.rsqrt(jnp.mean(centred * centred, -1, keepdims=True) + epsilon)
+    return centred * scale, scale
+
+
+def normal_pull(grad, unit, scale):
+    return scale * (
+        grad - jnp.mean(grad, -1, keepdims=True) - unit * jnp.mean(grad * unit, -1, keepdims=True)
+    )
 
 
 def forward_kernel(
     lengths, views, x_ref, gain_ref, pad_ref, wq_ref, wkv_ref,
-    normed, qa, ka, va, o_ref, received,
-    weight, stage, scores, tail, peak, acc, outgoing,
-    sib_send, sib_recv, line_send, line_recv, out_send, out_recv,
+    normed_out, qa_out, ka_out, va_out, o_out, received,
+    normed, qa, ka, va, o_ref, weight, stage, peak, outgoing,
+    sib_send, sib_recv, line_send, line_recv, out_send, out_recv, store,
 ):
     rows, width = x_ref.shape[1], x_ref.shape[2]
     blocks = normed.shape[0]
@@ -118,16 +170,28 @@
     sibling = me + 1 - 2 * core
     lane = lax.broadcasted_iota(jnp.int32, (rows, LANES), 1)
 
-    greet_line(dp, me, blocks)
+    arrived = greet(dp, me, blocks)
+    gain = gain_ref[...].reshape(1, width)
 
     def norm(value):
-        value = value.astype(f32)
-        mean = jnp.mean(value, -1, keepdims=True)
-        centred = value - mean
-        var = jnp.mean(centred * centred, -1, keepdims=True)
-        return (centred * lax.rsqrt(var + epsilon) * gain_ref[...]).astype(bf16)
+        return (normal(value.astype(f32))[0] * gain).astype(bf16)
 
     normed[me] = norm(x_ref[core])
+    arrived()
+
+    def place(block):
+        return pl.ds(pl.multiple_of(block * rows, rows), rows)
+
+    def keep(block, number):
+        here = place(block)
+        src, dst = (
+            (normed.at[block], normed_out.at[block // 2, pl.ds(pl.multiple_of(lax.rem(block, 2) * rows, rows), rows)]),
+            (ka.at[:, here, :], ka_out.at[:, here, :]),
+            (va.at[:, here, :], va_out.at[:, here, :]),
+            (qa.at[:, here, :], qa_out.at[:, here, :]),
+            (outgoing.at[block], o_out.at[block]),
+        )[number]
+        return pltpu.make_async_copy(src, dst, store.at[block, number])
 
     def line_copy(block, up):
         return pltpu.make_async_remote_copy(
@@ -177,12 +241,11 @@
 
     ones = jnp.where((lane >= HEAD) & (lane < HEAD + 3), -1.0, 0.0)
 
-    @pl.loop(0, blocks)
-    def _(step):
-        chip = chip_order(z, step // 2)
-        block = 2 * chip + lax.rem(core + step, 2)
-
-        @pl.when(step == 1)
+    def bring(step, turn):
+        chip = chip_order(z, step)
+        block = 2 * chip + lax.rem(core + turn, 2)
+
+        @pl.when((step == 0) & (turn == 1))
         def _():
             pltpu.make_async_remote_copy(
                 src_ref=stage,
@@ -193,7 +256,7 @@
                 device_id_type=MESH,
             ).wait_recv()
 
-        @pl.when(step > 1)
+        @pl.when(step > 0)
         def _():
             pltpu.make_async_remote_copy(
                 src_ref=normed.at[block],
@@ -204,15 +267,16 @@
                 device_id_type=MESH,
             ).wait_recv()
 
-        @pl.when((step > 0) & (chip <= z) & (z < 3))
+        @pl.when((step + turn > 0) & (chip <= z) & (z < 3))
         def _():
             line_copy(block, 1).start()
 
-        @pl.when((step > 0) & (chip >= z) & (z > 0))
+        @pl.when((step + turn > 0) & (chip >= z) & (z > 0))
         def _():
             line_copy(block, 0).start()
 
-        pad_row = 1.0 - pad_ref[core, pl.ds(block, 1), :].astype(f32)
+        keep(block, 0).start()
+        pad_row = 1.0 - pad_ref[pl.ds(core, 1), place(block)].astype(f32)
         padded = jnp.transpose(jnp.broadcast_to(pad_row, (LANES, rows)))
         key, query = features(block, rows, lengths, views, core, padded)
         out = dot_nn(normed[block], weight[...]).astype(bf16).astype(f32)
@@ -222,11 +286,36 @@
             qa[head, here, :] = (out[:, at : at + LANES] * (HEAD**-0.5) + query).astype(bf16)
             ka[head, here, :] = (out[:, at + LANES : at + 2 * LANES] + key).astype(bf16)
             va[head, here, :] = (out[:, at + 2 * LANES : at + 3 * LANES] + ones).astype(bf16)
-
-    eye = lax.broadcasted_iota(jnp.int32, (rows, rows), 0) == lax.broadcasted_iota(
-        jnp.int32, (rows, rows), 1
+            peak[head, here, :] = jnp.full((rows, LANES), -BIG, f32)
+            o_ref[head, here, :] = jnp.zeros((rows, LANES), f32)
+        keep(block, 1).start()
+        keep(block, 2).start()
+
+    wide = 2 * rows
+    eye = lax.broadcasted_iota(jnp.int32, (wide, wide), 0) == lax.broadcasted_iota(
+        jnp.int32, (wide, wide), 1
     )
-    half = LANES
+
+    def attend(queries, keys, diagonal=False):
+        found = []
+        for head in range(heads):
+            query = qa[head, queries, :]
+            key = ka[head, keys, :]
+            s = dot_nt(query, key)
+            if diagonal:
+                s = jnp.where(eye, dot_nt(query[:, :HEAD], key[:, :HEAD]), s)
+            tiles = [s[:, i : i + LANES] for i in range(0, s.shape[1], LANES)]
+            top = tiles[0]
+            for tile in tiles[1:]:
+                top = jnp.maximum(top, tile)
+            old = peak[head, queries, :]
+            new = jnp.maximum(old, jnp.max(top, -1, keepdims=True))
+            p = jnp.concatenate([jnp.exp(tile - new).astype(bf16) for tile in tiles], 1)
+            total = o_ref[head, queries, :] * jnp.exp(old - new) + dot_nn(p, va[head, keys, :])
+            found.append((new, total))
+        for head, (new, total) in enumerate(found):
+            peak[head, queries, :] = new
+            o_ref[head, queries, :] = total
 
     def out_copy(block):
         return pltpu.make_async_remote_copy(
@@ -238,77 +327,90 @@
             device_id_type=MESH,
         )
 
-    @pl.loop(0, blocks)
+    def hand_back(chip):
+        @pl.loop(0, 2)
+        def _(turn):
+            block = 2 * chip + lax.rem(core + turn, 2)
+            here = pl.ds(pl.multiple_of(block * rows, rows), rows)
+            results = []
+            for head in range(heads):
+                total = o_ref[head, here, :]
+                mass = -total[:, HEAD : HEAD + 1]
+                results.append((total / mass)[:, :HEAD].astype(bf16))
+                log_total = peak[head, here, :] + jnp.log(mass)
+                qa[head, here, :] = (
+                    qa[head, here, :].astype(f32) - spread(log_total, HEAD + CODES + 1, lane)
+                ).astype(bf16)
+            both, third = pack_heads(results)
+            outgoing[block, :rows, :] = both
+            outgoing[block, rows:, :] = third
+
+            @pl.when(block == me)
+            def _():
+                received[me, :rows, :] = both
+                received[me, rows:, :] = third
+
+            @pl.when(block != me)
+            def _():
+                out_copy(block).start()
+
+            keep(block, 3).start()
+            keep(block, 4).start()
+
+    def span(chip):
+        return pl.ds(pl.multiple_of(chip * wide, wide), wide)
+
+    def across(chip):
+        edge = (chip + 1) * wide
+        attend(
+            pl.ds(pl.multiple_of(edge - LANES, LANES), LANES),
+            pl.ds(pl.multiple_of(edge, LANES), LANES),
+        )
+
+    @pl.loop(0, blocks // 2)
     def _(step):
-        block = 2 * far_order(z, step // 2) + lax.rem(core + step, 2)
-        here = pl.ds(pl.multiple_of(block * rows, rows), rows)
-        last = block == blocks - 1
-        beyond = jnp.where(last, blocks * rows - half, (block + 1) * rows)
-        beyond = pl.ds(pl.multiple_of(beyond, half), half)
-        shut = jnp.where(last, -BIG, 0.0)
-        for head in range(heads):
-            query = qa[head, here, :]
-            s = dot_nt(query, ka[head, here, :])
-            plain = dot_nt(query[:, :HEAD], ka[head, here, :HEAD])
-            s = jnp.where(eye, plain, s)
-            t = dot_nt(query, ka[head, beyond, :]) + shut
-            scores[block, head] = s
-            tail[head] = t
-            peak[head] = jnp.maximum(jnp.maximum(s[:, :LANES], s[:, LANES:]), t)
-
-        @pl.loop(0, block)
+        @pl.loop(0, 2)
+        def _(turn):
+            bring(step, turn)
+
+        chip = chip_order(z, step)
+        low, high = chip_span(z, step)
+
+        @pl.when(chip > low)
+        def _():
+            across(chip - 1)
+
+        @pl.when(chip < high)
+        def _():
+            across(chip)
+
+        @pl.when((low == 0) & (chip == high) & (chip > 0))
+        def _():
+            hand_back(chip - 1)
+
+        @pl.loop(low, high + 1)
         def _(other):
-            there = pl.ds(pl.multiple_of(other * rows, rows), rows)
-            for head in range(heads):
-                s = dot_nt(qa[head, here, :], ka[head, there, :])
-                scores[other, head] = s
-                peak[head] = jnp.maximum(peak[head], jnp.maximum(s[:, :LANES], s[:, LANES:]))
-
-        for head in range(heads):
-            top = jnp.max(peak[head], -1, keepdims=True)
-            peak[head] = jnp.broadcast_to(top, (rows, LANES))
-            p = jnp.exp(tail[head] - top).astype(bf16)
-            acc[head] = dot_nn(p, va[head, beyond, :])
-
-        @pl.loop(0, block + 1)
-        def _(other):
-            there = pl.ds(pl.multiple_of(other * rows, rows), rows)
-            for head in range(heads):
-                top = peak[head]
-                s = scores[other, head]
-                p = jnp.concatenate(
-                    [jnp.exp(s[:, :LANES] - top), jnp.exp(s[:, LANES:] - top)], 1
-                ).astype(bf16)
-                acc[head] += dot_nn(p, va[head, there, :])
-
-        results = []
-        for head in range(heads):
-            total = acc[head]
-            mass = -total[:, HEAD : HEAD + 1]
-            out = total / mass
-            o_ref[head, here, :] = out
-            results.append(out[:, :HEAD].astype(bf16))
-            log_total = peak[head] + jnp.log(mass)
-            qa[head, here, :] = (
-                qa[head, here, :].astype(f32) - spread(log_total, HEAD + CODES + 1, lane)
-            ).astype(bf16)
-        wide, narrow = pack_heads(results)
-
-        @pl.when(block == me)
-        def _():
-            received[me, :rows, :] = wide
-            received[me, rows:, :] = narrow
-
-        @pl.when(block != me)
-        def _():
-            outgoing[block, :rows, :] = wide
-            outgoing[block, rows:, :] = narrow
-            out_copy(block).start()
+            top = jnp.maximum(chip, other)
+
+            @pl.when(other == chip)
+            def _():
+                attend(span(chip), span(chip), True)
+
+            @pl.when(other != chip)
+            def _():
+                attend(span(top), span(jnp.minimum(chip, other)))
+
+            @pl.when((other >= chip) & (low == 0) & (high >= jnp.minimum(top + 1, blocks // 2 - 1)))
+            def _():
+                hand_back(top)
 
     sib_copy.wait_send()
 
     @pl.loop(0, blocks)
     def _(block):
+        for number in range(5):
+            keep(block, number).wait()
+
         @pl.when((block // 2 <= z) & (z < 3))
         def _():
             line_copy(block, 1).wait_send()
@@ -330,28 +432,436 @@
             ).wait_recv()
 
 
+class Sums:
+    def __init__(self, final, own, buffers, semaphores, local):
+        self.final, self.own, self.local = final, own, local
+        self.from_core, self.first, self.second, self.line, self.near, self.far = buffers
+        self.sems = dict(zip(
+            ("core", "first", "second", "inward", "across", "outward", "back", "wide", "twin"), semaphores
+        ))
+        self.count = own.shape[0]
+        self.half, self.lanes = own.shape[1], own.shape[2]
+        self.quarter = self.half // 4
+        self.eighth = self.half // 8
+        self.dp = lax.axis_index("dp")
+        self.me = lax.axis_index("blk")
+        self.core = lax.rem(self.me, 2)
+        self.z = self.me // 2
+        self.x = lax.rem(self.dp, 2)
+        self.y = self.dp // 2
+        self.along_x = (self.dp + 1 - 2 * self.x, self.me)
+        self.along_y = (self.dp + 2 - 4 * self.y, self.me)
+        self.twin = (self.dp, self.me + 1 - 2 * self.core)
+        self.inner = (self.z == 1) | (self.z == 2)
+        self.outer = (self.z == 0) | (self.z == 3)
+        self.pair = (self.dp, self.me + 2 - 4 * lax.rem(self.z, 2))
+        self.middle = (self.dp, jnp.where(self.z < 2, self.me + 2, self.me - 2))
+
+    def copy(self, name, piece, src, dst, device, way=None):
+        send, recv = self.sems[name]
+        at = (piece,) if way is None else (piece, way)
+        return pltpu.make_async_remote_copy(
+            src_ref=src,
+            dst_ref=dst,
+            send_sem=send.at[at],
+            recv_sem=recv.at[at],
+            device_id=device,
+            device_id_type=MESH,
+        )
+
+    def rows(self, start, count):
+        return pl.ds(pl.multiple_of(start, 16), count)
+
+    def place(self, ref, piece, start, count):
+        cols = pl.ds(pl.multiple_of(lax.rem(piece, 2) * self.lanes, LANES), self.lanes)
+        return ref.at[piece // 2, self.rows(start, count), cols]
+
+    def to_core(self, piece, src=None):
+        src = self.own.at[piece] if src is None else src
+        return self.copy("core", piece, src, self.from_core.at[piece], self.twin)
+
+    def to_first(self, piece):
+        q = self.quarter
+        return (
+            self.copy("first", piece, self.own.at[piece, self.rows(q * (1 - self.x), q)], self.first.at[piece, 0], self.along_x, 0),
+            self.copy("first", piece, self.own.at[piece, self.rows(2 * q + q * (1 - self.y), q)], self.first.at[piece, 1], self.along_y, 1),
+        )
+
+    def to_second(self, piece):
+        q, e = self.quarter, self.eighth
+        return (
+            self.copy("second", piece, self.own.at[piece, self.rows(q * self.x + e * (1 - self.y), e)], self.second.at[piece, 0], self.along_y, 0),
+            self.copy("second", piece, self.own.at[piece, self.rows(2 * q + q * self.y + e * (1 - self.x), e)], self.second.at[piece, 1], self.along_x, 1),
+        )
+
+    def inward(self, piece):
+        return self.copy("inward", piece, self.line.at[piece], self.near.at[piece], self.pair)
+
+    def across(self, piece):
+        return self.copy("across", piece, self.line.at[piece], self.far.at[piece], self.middle)
+
+    def outward(self, piece):
+        return self.copy("outward", piece, self.far.at[piece], self.near.at[piece], self.pair)
+
+    def mine(self):
+        q, e = self.quarter, self.eighth
+        base = self.core * self.half
+        return base + q * self.x + e * self.y, base + 2 * q + q * self.y + e * self.x
+
+    def keep(self, piece, total):
+        e = self.eighth
+        one, two = self.mine()
+        return (
+            pltpu.make_async_copy(total.at[piece, :e], self.place(self.final, piece, one, e), self.local.at[piece, 0]),
+            pltpu.make_async_copy(total.at[piece, e:], self.place(self.final, piece, two, e), self.local.at[piece, 1]),
+        )
+
+    def back(self, piece, total):
+        e = self.eighth
+        one, two = self.mine()
+        return (
+            self.copy("back", piece, total.at[piece, :e], self.place(self.final, piece, one, e), self.along_y, 0),
+            self.copy("back", piece, total.at[piece, e:], self.place(self.final, piece, two, e), self.along_x, 1),
+        )
+
+    def wide(self, piece):
+        q = self.quarter
+        base = self.core * self.half
+        one = self.place(self.final, piece, base + q * self.x, q)
+        two = self.place(self.final, piece, base + 2 * q + q * self.y, q)
+        return (
+            self.copy("wide", piece, one, one, self.along_x, 0),
+            self.copy("wide", piece, two, two, self.along_y, 1),
+        )
+
+    def to_twin(self, piece):
+        part = self.place(self.final, piece, self.core * self.half, self.half)
+        return self.copy("twin", piece, part, part, self.twin)
+
+    def step_1(self, piece):
+        self.to_core(piece).wait_recv()
+        self.own[piece] = self.own[piece] + self.from_core[piece]
+        for copy in self.to_first(piece):
+            copy.start()
+
+    def step_2(self, piece):
+        q = self.quarter
+        one, two = self.to_first(piece)
+        one.wait_recv()
+        at = self.rows(q * self.x, q)
+        self.own[piece, at, :] = self.own[piece, at, :] + self.first[piece, 0]
+        two.wait_recv()
+        at = self.rows(2 * q + q * self.y, q)
+        self.own[piece, at, :] = self.own[piece, at, :] + self.first[piece, 1]
+        for copy in self.to_second(piece):
+            copy.start()
+
+    def step_3(self, piece):
+        q, e = self.quarter, self.eighth
+        one, two = self.to_second(piece)
+        one.wait_recv()
+        at = self.rows(q * self.x + e * self.y, e)
+        self.line[piece, :e, :] = self.own[piece, at, :] + self.second[piece, 0]
+        two.wait_recv()
+        at = self.rows(2 * q + q * self.y + e * self.x, e)
+        self.line[piece, e:, :] = self.own[piece, at, :] + self.second[piece, 1]
+
+        @pl.when(self.outer)
+        def _():
+            self.inward(piece).start()
+
+    def step_4(self, piece):
+        @pl.when(self.inner)
+        def _():
+            self.inward(piece).wait_recv()
+            self.line[piece] = self.line[piece] + self.near[piece]
+            self.across(piece).start()
+
+    def step_5(self, piece):
+        @pl.when(self.inner)
+        def _():
+            self.across(piece).wait_recv()
+            self.far[piece] = self.line[piece] + self.far[piece]
+            self.outward(piece).start()
+
+    def step_6(self, piece):
+        @pl.when(self.outer)
+        def _():
+            self.outward(piece).wait_recv()
+            for copy in self.back(piece, self.near) + self.keep(piece, self.near):
+                copy.start()
+
+        @pl.when(self.inner)
+        def _():
+            for copy in self.back(piece, self.far) + self.keep(piece, self.far):
+                copy.start()
+
+    def step_7(self, piece):
+        for copy in self.keep(piece, self.near):
+            copy.wait()
+        for copy in self.back(piece, self.near):
+            copy.wait_recv()
+        for copy in self.wide(piece):
+            copy.start()
+
+    def step_8(self, piece):
+        for copy in self.wide(piece):
+            copy.wait_recv()
+        self.to_twin(piece).start()
+
+    def step_9(self, piece):
+        self.to_twin(piece).wait_recv()
+
+    def tick(self, numbers, offsets, time, last):
+        for place in reversed(range(len(numbers))):
+            piece = time - offsets[place]
+
+            @pl.when((piece >= 0) & (piece < last))
+            def _():
+                getattr(self, "step_" + str(numbers[place]))(piece)
+
+    def finish(self, piece):
+        for copies in (self.to_first(piece), self.to_second(piece), self.back(piece, self.near), self.wide(piece)):
+            for copy in copies:
+                copy.wait_send()
+        self.to_twin(piece).wait_send()
+
+        @pl.when(self.outer)
+        def _():
+            self.inward(piece).wait_send()
+
+        @pl.when(self.inner)
+        def _():
+            self.across(piece).wait_send()
+            self.outward(piece).wait_send()
+
+    @staticmethod
+    def scratch(count, half, lanes):
+        def array(*shape):
+            return pltpu.VMEM((count,) + shape + (lanes,), bf16)
+
+        quarter, eighth = half // 4, half // 8
+        dma = pltpu.SemaphoreType.DMA
+        one, two = [dma((count,))] * 2, [dma((count, 2))] * 2
+        return (
+            [array(half)] * 2
+            + [array(2, quarter), array(2, eighth)]
+            + [array(quarter)] * 3
+            + one + two + two + one + one + one + two + two + one
+            + [dma((count, 2))]
+        )
+
+    @classmethod
+    def gather(cls, final, refs):
+        sems = refs[7:25]
+        pairs = [(sems[2 * i], sems[2 * i + 1]) for i in range(9)]
+        return cls(final, refs[0], refs[1:7], pairs, refs[25])
+
+
+class UnitSum:
+    def __init__(self, sums, final, refs):
+        self.sums, self.final = sums, final
+        (
+            self.own, self.give, self.from_core, self.first, self.second, self.line,
+            self.core_sems, self.first_sems, self.second_sems, self.line_send, self.line_recv,
+            self.back_sems, self.wide_sems, self.twin_sems, self.local,
+        ) = refs
+
+    def copy(self, sems, at, src, dst, device):
+        return pltpu.make_async_remote_copy(
+            src_ref=src,
+            dst_ref=dst,
+            send_sem=sems.at[0, at],
+            recv_sem=sems.at[1, at],
+            device_id=device,
+            device_id_type=MESH,
+        )
+
+    def to_core(self):
+        return self.copy(self.core_sems, 0, self.give, self.from_core, self.sums.twin)
+
+    def to_first(self):
+        s, q = self.sums, self.sums.quarter
+        return (
+            self.copy(self.first_sems, 0, self.own.at[s.rows(q * (1 - s.x), q)], self.first.at[0], s.along_x),
+            self.copy(self.first_sems, 1, self.own.at[s.rows(2 * q + q * (1 - s.y), q)], self.first.at[1], s.along_y),
+        )
+
+    def to_second(self):
+        s, q, e = self.sums, self.sums.quarter, self.sums.eighth
+        return (
+            self.copy(self.second_sems, 0, self.own.at[s.rows(q * s.x + e * (1 - s.y), e)], self.second.at[0], s.along_y),
+            self.copy(self.second_sems, 1, self.own.at[s.rows(2 * q + q * s.y + e * (1 - s.x), e)], self.second.at[1], s.along_x),
+        )
+
+    def along_line(self, chip):
+        s = self.sums
+        return pltpu.make_async_remote_copy(
+            src_ref=self.line.at[s.z],
+            dst_ref=self.line.at[s.z],
+            send_sem=self.line_send.at[chip],
+            recv_sem=self.line_recv.at[s.z],
+            device_id=(s.dp, 2 * chip + s.core),
+            device_id_type=MESH,
+        )
+
+    def from_line(self, chip):
+        s = self.sums
+        return pltpu.make_async_remote_copy(
+            src_ref=self.line.at[chip],
+            dst_ref=self.line.at[chip],
+            send_sem=self.line_send.at[chip],
+            recv_sem=self.line_recv.at[chip],
+            device_id=(s.dp, 2 * chip + s.core),
+            device_id_type=MESH,
+        )
+
+    def keep(self):
+        s, e = self.sums, self.sums.eighth
+        one, two = s.mine()
+        return (
+            pltpu.make_async_copy(self.line.at[:, :e], self.final.at[:, s.rows(one, e)], self.local.at[0]),
+            pltpu.make_async_copy(self.line.at[:, e:], self.final.at[:, s.rows(two, e)], self.local.at[1]),
+        )
+
+    def back(self):
+        s, e = self.sums, self.sums.eighth
+        one, two = s.mine()
+        return (
+            self.copy(self.back_sems, 0, self.line.at[:, :e], self.final.at[:, s.rows(one, e)], s.along_y),
+            self.copy(self.back_sems, 1, self.line.at[:, e:], self.final.at[:, s.rows(two, e)], s.along_x),
+        )
+
+    def wide(self):
+        s, q = self.sums, self.sums.quarter
+        base = s.core * s.half
+        one = self.final.at[:, s.rows(base + q * s.x, q)]
+        two = self.final.at[:, s.rows(base + 2 * q + q * s.y, q)]
+        return (
+            self.copy(self.wide_sems, 0, one, one, s.along_x),
+            self.copy(self.wide_sems, 1, two, two, s.along_y),
+        )
+
+    def to_twin(self):
+        s = self.sums
+        part = self.final.at[:, s.rows(s.core * s.half, s.half)]
+        return self.copy(self.twin_sems, 0, part, part, s.twin)
+
+    def step(self, number):
+        s, q, e = self.sums, self.sums.quarter, self.sums.eighth
+        if number == 0:
+            self.to_core().start()
+        elif number == 1:
+            self.to_core().wait_recv()
+            self.own[...] = self.own[...] + self.from_core[...]
+            for copy in self.to_first():
+                copy.start()
+        elif number == 2:
+            for way, start in ((0, q * s.x), (1, 2 * q + q * s.y)):
+                self.to_first()[way].wait_recv()
+                at = s.rows(start, q)
+                self.own[at, :] = self.own[at, :] + self.first[way]
+            for copy in self.to_second():
+                copy.start()
+        elif number == 3:
+            for way, start in ((0, q * s.x + e * s.y), (1, 2 * q + q * s.y + e * s.x)):
+                self.to_second()[way].wait_recv()
+                self.line[s.z, way * e : (way + 1) * e, :] = self.own[s.rows(start, e), :] + self.second[way]
+            for ahead in (2, 1, 3):
+                self.along_line(lax.rem(s.z + ahead, 4)).start()
+        elif number == 4:
+            for ahead in (1, 2, 3):
+                self.from_line(lax.rem(s.z + ahead, 4)).wait_recv()
+            for copy in self.back() + self.keep():
+                copy.start()
+        elif number == 5:
+            for copy in self.keep():
+                copy.wait()
+            for copy in self.back():
+                copy.wait_recv()
+            for copy in self.wide():
+                copy.start()
+        elif number == 6:
+            for copy in self.wide():
+                copy.wait_recv()
+            self.to_twin().start()
+        else:
+            self.to_twin().wait_recv()
+
+    def finish(self):
+        s = self.sums
+        for copy in (self.to_core(), self.to_twin()) + self.to_first() + self.to_second() + self.back() + self.wide():
+            copy.wait_send()
+        for ahead in (1, 2, 3):
+            self.along_line(lax.rem(s.z + ahead, 4)).wait_send()
+
+    @staticmethod
+    def scratch(chips, half, lanes):
+        dma = pltpu.SemaphoreType.DMA
+        quarter, eighth = half // 4, half // 8
+        array = [pltpu.VMEM((half, lanes), bf16)]
+        return (
+            array * 3
+            + [
+                pltpu.VMEM((2, quarter, lanes), bf16),
+                pltpu.VMEM((2, eighth, lanes), bf16),
+                pltpu.VMEM((chips, quarter, lanes), bf16),
+                dma((2, 1)),
+                dma((2, 2)),
+                dma((2, 2)),
+                dma((chips,)),
+                dma((chips,)),
+                dma((2, 2)),
+                dma((2, 2)),
+                dma((2, 1)),
+                dma((2,)),
+            ]
+        )
+
+
 def backward_kernel(
-    grad_ref, normed, qa, ka, va, o_ref,
-    got_query, got_pair, grad_weight,
-    outgoing, received, doa, dq, dk, dv, mine, send_query, send_pair,
-    out_send, out_recv, query_send, query_recv, pair_send, pair_recv,
+    grad_ref, mixed_grad_ref, gain_ref, acts_in, normed_in, qa_in, ka_in, va_in, o_in, wq_in, wkv_in, x_in,
+    input_grad, final, unit_final,
+    acts, qa, ka, va, out, received, doa, right_key, key_turned, dqt, dvk, send_query, send_pair,
+    got_query, got_pair, unit, give,
+    load_acts, load_heads, load_late, out_send, out_recv, query_send, query_recv, pair_send, pair_recv,
+    *sum_refs,
 ):
-    rows, width = grad_ref.shape[1], grad_ref.shape[2]
-    blocks = normed.shape[0]
+    blocks, packed = grad_ref.shape[0], grad_ref.shape[1]
+    rows = 2 * packed // 3
+    micro, _, width = input_grad.shape
     heads = qa.shape[0]
+    chips = blocks // 2
     dp = lax.axis_index("dp")
     me = lax.axis_index("blk")
     z = me // 2
     core = lax.rem(me, 2)
     lane = lax.broadcasted_iota(jnp.int32, (rows, LANES), 1)
-    greet_line(dp, me, blocks)
+    sums = Sums.gather(final, sum_refs[:26])
+    units = UnitSum(sums, unit_final, sum_refs[26:])
+    count = sums.count
+    arrived = greet(dp, me, blocks, (sums.along_x, sums.along_y))
+
+    def load(block):
+        return pltpu.make_async_copy(acts_in.at[block], acts.at[block], load_acts.at[block])
+
+    def load_head(number):
+        src = (qa_in, ka_in, va_in, o_in)[number]
+        return pltpu.make_async_copy(src, (qa, ka, va, out)[number], load_heads.at[number])
+
+    order = [9, 0, 1, 2, 3, 8, 4, 5, 6, 7, 10, 11]
+    for block in order[:3]:
+        load(block).start()
+    arrived()
+
+    kinds = {
+        "grad": (grad_ref, received, out_send, out_recv),
+        "query": (send_query, got_query, query_send, query_recv),
+        "pair": (send_pair, got_pair, pair_send, pair_recv),
+    }
 
     def send(kind, block):
-        src, dst, send_sem, recv_sem = {
-            "grad": (outgoing, received, out_send, out_recv),
-            "query": (send_query, got_query, query_send, query_recv),
-            "pair": (send_pair, got_pair, pair_send, pair_recv),
-        }[kind]
+        src, dst, send_sem, recv_sem = kinds[kind]
         return pltpu.make_async_remote_copy(
             src_ref=src.at[block],
             dst_ref=dst.at[me],
@@ -362,11 +872,7 @@
         )
 
     def arrive(kind, block):
-        src, dst, send_sem, recv_sem = {
-            "grad": (outgoing, received, out_send, out_recv),
-            "query": (send_query, got_query, query_send, query_recv),
-            "pair": (send_pair, got_pair, pair_send, pair_recv),
-        }[kind]
+        src, dst, send_sem, recv_sem = kinds[kind]
         return pltpu.make_async_remote_copy(
             src_ref=src.at[block],
             dst_ref=dst.at[block],
@@ -376,15 +882,6 @@
             device_id_type=MESH,
         )
 
-    for chip in range(blocks // 2):
-        for row in range(2):
-            at = chip * heads * HEAD
-            wide, narrow = pack_heads(
-                [grad_ref[row, :, at + h * HEAD : at + (h + 1) * HEAD] for h in range(heads)]
-            )
-            outgoing[2 * chip + row, :rows, :] = wide
-            outgoing[2 * chip + row, rows:, :] = narrow
-
     for step in range(4):
         for row in range(2):
             block = 2 * far_order(z, jnp.int32(step)) + row
@@ -393,7 +890,109 @@
             def _():
                 send("grad", block).start()
 
-    received[me] = outgoing[me]
+    for block in order[3:]:
+        load(block).start()
+    for number in range(4):
+        load_head(number).start()
+    received[me] = grad_ref[me]
+
+    def message(number):
+        return 2 * far_order(z, number // 2) + lax.rem(core + number, 2)
+
+    def slot(time):
+        for kind, starts in (("pair", PAIR_SLOTS), ("query", QUERY_SLOTS)):
+            for number, start in enumerate(starts):
+                block = message(jnp.int32(2 * chips - 1 if number == 2 * chips - 2 else number))
+
+                @pl.when(time == start)
+                def _():
+                    send(kind, block).start()
+
+        sums.tick(OUT, OUT_AT, time, count)
+        sums.tick(BACK, BACK_AT, time - LATE, count)
+
+    parts = (count // 2 - 1) // 2
+    side = sums.half
+
+    def weigh(piece):
+        whole = piece // 2
+        left = jnp.where(whole < parts, whole, jnp.where(whole < 2 * parts, 2 * parts, 2 * parts + 2))
+        right = jnp.where(whole < parts, 2 * parts + 1, jnp.where(whole < 2 * parts, whole, 2 * parts + 3))
+        cols = pl.ds(pl.multiple_of(lax.rem(piece, 2) * side, LANES), side)
+        turn = lax.rem(piece, GIVE)
+
+        @pl.when(piece >= GIVE)
+        def _():
+            sums.to_core(piece - GIVE, give.at[turn]).wait_send()
+
+        operand = acts[right, :, cols]
+        theirs = pl.ds(pl.multiple_of((1 - core) * side, LANES), side)
+        give[turn] = dot_tn(acts[left, :, theirs], operand).astype(bf16)
+        sums.to_core(piece, give.at[turn]).start()
+        ours = pl.ds(pl.multiple_of(core * side, LANES), side)
+        sums.own[piece] = dot_tn(acts[left, :, ours], operand).astype(bf16)
+
+    per_slot = count // EARLY
+    for number in range(EARLY):
+        if number == 0:
+            for block in order[:5]:
+                load(block).wait()
+        if number == 2:
+            for block in order[5:]:
+                load(block).wait()
+
+        @pl.loop(0, per_slot)
+        def _(turn):
+            weigh(number * per_slot + turn)
+
+        slot(jnp.int32(number))
+
+    squares = [(wq_in, 0), (wkv_in, 0), (wkv_in, width)]
+    tall = acts.shape[1]
+
+    def late():
+        copies = [
+            pltpu.make_async_copy(normed_in.at[chip], acts.at[chip], load_late.at[chip]) for chip in range(chips)
+        ]
+        for number, (src, start) in enumerate(squares):
+            cols = pl.ds(start, width)
+            copies.append(
+                pltpu.make_async_copy(
+                    src.at[pl.ds(0, tall), cols], acts.at[chips + 2 * number], load_late.at[chips + 2 * number]
+                )
+            )
+            copies.append(
+                pltpu.make_async_copy(
+                    src.at[pl.ds(tall, width - tall), cols],
+                    acts.at[chips + 2 * number + 1, pl.ds(0, width - tall)],
+                    load_late.at[chips + 2 * number + 1],
+                )
+            )
+        for row in range(micro):
+            copies.append(
+                pltpu.make_async_copy(
+                    x_in.at[row],
+                    acts.at[chips + 6, pl.ds(row * rows, rows)],
+                    load_late.at[chips + 6 + row],
+                )
+            )
+        return copies
+
+    for copy in late():
+        copy.start()
+
+    dqt[...] = jnp.zeros_like(dqt)
+    for number in range(4):
+        load_head(number).wait()
+
+    @pl.loop(0, blocks)
+    def _(block):
+        here = pl.ds(pl.multiple_of(block * rows, rows), rows)
+        for head in range(heads):
+            key = ka[head, here, :][:, :HEAD].astype(f32)
+            key_turned[head, :, here] = jnp.transpose(key).astype(bf16)
+            query = qa[head, here, :][:, :HEAD]
+            right_key[head, here, :] = jnp.concatenate([jnp.zeros_like(query), query], 1)
 
     @pl.loop(0, blocks)
     def _(step):
@@ -406,123 +1005,331 @@
         here = pl.ds(pl.multiple_of(block * rows, rows), rows)
         wide = received[block, :rows, :].astype(f32)
         narrow = received[block, rows:, :].astype(f32)
-        pieces = [
-            wide[:, :HEAD],
-            wide[:, HEAD:],
-            jnp.concatenate([narrow[:, :HEAD], narrow[:, HEAD:]], 0),
-        ]
+        shares = heads_of(wide * out[block, :rows, :].astype(f32), narrow * out[block, rows:, :].astype(f32))
         gap = jnp.zeros((rows, LANES - HEAD), f32)
+        for head, piece in enumerate(heads_of(wide, narrow)):
+            delta = jnp.sum(shares[head], -1, keepdims=True)
+            value = jnp.concatenate([piece, gap], 1)
+            doa[head, here, :] = (value + spread(delta, HEAD, lane)).astype(bf16)
+
+    wide_rows = 2 * rows
+    eye = lax.broadcasted_iota(jnp.int32, (wide_rows, wide_rows), 0) == lax.broadcasted_iota(
+        jnp.int32, (wide_rows, wide_rows), 1
+    )
+    half = LANES
+
+    def pull(keys, queries, diagonal=False):
+        found = []
         for head in range(heads):
-            value = jnp.concatenate([pieces[head], gap], 1)
-            delta = jnp.sum(value * o_ref[head, here, :], -1, keepdims=True)
-            doa[head, here, :] = (value + spread(delta, HEAD, lane)).astype(bf16)
-            dq[head, here, :] = jnp.zeros((rows, LANES), f32)
-
-    eye = lax.broadcasted_iota(jnp.int32, (rows, rows), 0) == lax.broadcasted_iota(
-        jnp.int32, (rows, rows), 1
-    )
-    bare = (lane < HEAD) | (lane > HEAD + CODES)
-    half = LANES
-
-    def pull(head, keys, queries, diagonal, first):
-        k = ka[head, keys, :]
-        q = qa[head, queries, :]
-        g = doa[head, queries, :]
-        s = dot_nt(k, q)
-        if diagonal:
-            s = jnp.where(eye, dot_nt(jnp.where(bare, k, 0.0).astype(bf16), q), s)
-        p = jnp.exp(s)
-        ds = (p * dot_nt(va[head, keys, :], g)).astype(bf16)
-        p = p.astype(bf16)
-        count = k.shape[0]
-        if first:
-            dv[head] = dot_nn(p, g)
-            dk[head] = dot_nn(ds, q)
-        else:
-            dv[head, :count] += dot_nn(p, g)
-            dk[head, :count] += dot_nn(ds, q)
-        dq[head, queries, :] += dot_tn(ds, k)
+            k = ka[head, keys, :]
+            q = qa[head, queries, :]
+            g = doa[head, queries, :]
+            at = lax.broadcasted_iota(jnp.int32, k.shape, 1)
+            s = dot_nt(k, q)
+            if diagonal:
+                bare = (at < HEAD) | (at > HEAD + CODES)
+                s = jnp.where(eye, dot_nt(jnp.where(bare, k, 0.0).astype(bf16), q), s)
+            p = jnp.exp(s)
+            ds = (p * dot_nt(va[head, keys, :], g)).astype(bf16)
+            left = jnp.concatenate([p.astype(bf16), ds], 1)
+            at = lax.broadcasted_iota(jnp.int32, g.shape, 1)
+            value = jnp.where(at < HEAD, g, 0.0).astype(bf16)
+            right = jnp.concatenate([value, right_key[head, queries, :]], 0)
+            found.append((dot_nn(left, right), dot_nn(key_turned[head, :, keys], ds)))
+        return found
+
+    @pl.loop(0, chips)
+    def _(step):
+        chip = far_order(z, step)
+        here = pl.ds(pl.multiple_of(chip * wide_rows, wide_rows), wide_rows)
+        for head, (pair, query) in enumerate(pull(here, here, True)):
+            dvk[head] = pair
+            dqt[head, :, here] += query
+        time = EARLY
+        for earlier in range(chips - 1):
+            done = far_order(z, earlier)
+            bodies = chips - done + jnp.where(done > 0, 1, 0)
+            time = time + jnp.where(earlier < step, bodies, 0)
+        slot(time)
+
+        @pl.loop(chip + 1, chips)
+        def _(other):
+            there = pl.ds(pl.multiple_of(other * wide_rows, wide_rows), wide_rows)
+            for head, (pair, query) in enumerate(pull(here, there)):
+                dvk[head] += pair
+                dqt[head, :, there] += query
+            slot(time + other - chip)
+
+        @pl.when(chip > 0)
+        def _():
+            edge = chip * wide_rows
+            keys = pl.ds(pl.multiple_of(edge, half), half)
+            queries = pl.ds(pl.multiple_of(edge - half, half), half)
+            for head, (pair, query) in enumerate(pull(keys, queries)):
+                dvk[head, :half] += pair
+                dqt[head, :, queries] += query
+            slot(time + chips - chip)
+
+        for turn in range(2):
+            block = 2 * chip + turn
+            for head in range(heads):
+                send_pair[block, head * rows : (head + 1) * rows, :] = dvk[
+                    head, turn * rows : (turn + 1) * rows
+                ].astype(bf16)
+
+            @pl.when(block == me)
+            def _():
+                got_pair[me] = send_pair[me]
 
     @pl.loop(0, blocks)
     def _(step):
-        block = jnp.where(lax.rem(step, 2) == 0, step // 2, blocks - 1 - step // 2)
+        block = step
         here = pl.ds(pl.multiple_of(block * rows, rows), rows)
-        for head in range(heads):
-            pull(head, here, here, True, True)
-
-        @pl.loop(block + 1, blocks)
-        def _(other):
-            there = pl.ds(pl.multiple_of(other * rows, rows), rows)
+        wide, narrow = pack_heads(
+            [(jnp.transpose(dqt[h, :, here]) * (HEAD**-0.5)).astype(bf16) for h in range(heads)]
+        )
+        send_query[block, :rows, :] = wide
+        send_query[block, rows:, :] = narrow
+
+        @pl.when(block == me)
+        def _():
+            got_query[me] = send_query[me]
+
+    for copy in late():
+        copy.wait()
+
+    for turn in range(2):
+        which = 1 - core if turn == 0 else core
+        cols = pl.ds(pl.multiple_of(which * side, LANES), side)
+        unit[...] = jnp.zeros_like(unit)
+
+        @pl.loop(0, chips)
+        def _(chip):
+            tiles = []
+            for block in (2 * chip, 2 * chip + 1):
+                query = heads_of(send_query[block, :rows, :], send_query[block, rows:, :])
+                tile = [send_pair[block, head * rows : (head + 1) * rows, :] for head in range(heads)]
+                tile += query + [jnp.zeros((rows, LANES - HEAD), bf16)]
+                tiles.append(jnp.concatenate(tile, 1))
+            unit[...] += dot_tn(acts[chip, :, cols], jnp.concatenate(tiles, 0))
+
+        if turn == 0:
+            units.give[...] = unit[...].astype(bf16)
+            units.step(0)
+        else:
+            units.own[...] = unit[...].astype(bf16)
+        slot(jnp.int32(EARLY + 13 + turn))
+
+    ready = EARLY + 15
+    end = LATE + count + BACK_AT[-1]
+    spots = [int(ready + place) for place in UNIT_SLOTS]
+
+    def last(row):
+        query = columns_of(got_query, row, rows, blocks)
+        keys, values = [], []
+        for chip in range(chips):
             for head in range(heads):
-                pull(head, here, there, False, False)
-
-        @pl.when(block > 0)
-        def _():
-            keys = pl.ds(pl.multiple_of(block * rows, rows), half)
-            queries = pl.ds(pl.multiple_of(block * rows - half, half), half)
-            for head in range(heads):
-                pull(head, keys, queries, False, False)
-
-        for head in range(heads):
-            mine[head, here, :] = jnp.concatenate(
-                [dk[head][:, :HEAD], dv[head][:, :HEAD]], 1
-            ).astype(bf16)
-
-        @pl.when(block == me)
-        def _():
-            for head in range(heads):
-                got_pair[me, head * rows : (head + 1) * rows, :] = mine[head, here, :]
-
-        @pl.when(block != me)
-        def _():
-            for head in range(heads):
-                send_pair[block, head * rows : (head + 1) * rows, :] = mine[head, here, :]
-            send("pair", block).start()
-
-    @pl.loop(0, blocks)
-    def _(step):
-        block = 2 * far_order(z, step // 2) + lax.rem(core + step, 2)
-        here = pl.ds(pl.multiple_of(block * rows, rows), rows)
-        parts = [(dq[h, here, :][:, :HEAD] * (HEAD**-0.5)).astype(bf16) for h in range(heads)]
-        wide, narrow = pack_heads(parts)
-        mine[heads, here, :] = wide
-        mine[heads + 1, here, :] = jnp.concatenate(
-            [parts[2], jnp.zeros((rows, LANES - HEAD), bf16)], 1
-        )
-
-        @pl.when(block == me)
-        def _():
-            got_query[me, :rows, :] = wide
-            got_query[me, rows:, :] = narrow
-
-        @pl.when(block != me)
-        def _():
-            send_query[block, :rows, :] = wide
-            send_query[block, rows:, :] = narrow
-            send("query", block).start()
-
-    for tile in range(heads + 2):
-        grad_weight[:, tile * LANES : (tile + 1) * LANES] = jnp.zeros((width, LANES), f32)
-
-    @pl.loop(0, blocks)
-    def _(block):
-        here = pl.ds(pl.multiple_of(block * rows, rows), rows)
-        right = jnp.concatenate([mine[tile, here, :] for tile in range(heads + 2)], 1)
-        grad_weight[...] += dot_tn(normed[block], right)
+                both = got_pair[2 * chip + row, head * rows : (head + 1) * rows, :]
+                keys.append(both[:, HEAD:])
+                values.append(both[:, :HEAD])
+        grad = []
+        for part in range(2):
+            height = tall if part == 0 else width - tall
+            total = jnp.zeros((rows, height), f32)
+            for number, operand in enumerate(
+                (query, jnp.concatenate(keys, 1), jnp.concatenate(values, 1))
+            ):
+                total = total + dot_nt(operand, acts[chips + 2 * number + part, :height])
+            grad.append(total)
+        grad = jnp.concatenate(grad, 1)
+        unit_, scale = normal(acts[chips + 6, row * rows : (row + 1) * rows, :].astype(f32))
+        gain = gain_ref[...].reshape(1, width)
+        input_grad[row] = (mixed_grad_ref[row] + normal_pull(grad * gain, unit_, scale)).astype(bf16)
+
+    @pl.loop(ready, max(end, spots[-1] + 1, QUERY_SLOTS[-1] + 1))
+    def _(time):
+        for number, spot in enumerate(spots):
+
+            @pl.when(time == spot)
+            def _():
+                units.step(number + 1)
+
+        slot(time)
 
     @pl.loop(0, blocks)
     def _(block):
         @pl.when(block != me)
         def _():
+            arrive("query", block).wait_recv()
+            arrive("pair", block).wait_recv()
+
+    for row in range(micro):
+        last(row)
+
+    @pl.loop(0, blocks)
+    def _(block):
+        @pl.when(block != me)
+        def _():
             send("grad", block).wait_send()
             send("query", block).wait_send()
             send("pair", block).wait_send()
-            arrive("query", block).wait_recv()
-            arrive("pair", block).wait_recv()
+
+    for piece in range(count - GIVE, count):
+        sums.to_core(piece, give.at[piece % GIVE]).wait_send()
+
+    @pl.loop(0, count)
+    def _(piece):
+        sums.finish(piece)
+
+    units.finish()
+
+
+def dense_kernel(
+    received, x_ref, up_ref, gain_ref, wo_in, we_in, wc_in,
+    result_ref, mixed_grad_ref, attended_grad_ref, acts_out,
+    wo, we, wc, acts, mixed, result_acc, second_acc, load, store,
+):
+    micro, rows, width = x_ref.shape
+    blocks = received.shape[0]
+    parts = we.shape[0]
+    chips = blocks // 2
+    heads = width // HEAD // chips
+    fetch = [pltpu.make_async_copy(wo_in, wo, load.at[0])]
+    for part in range(parts):
+        cols = pl.ds(part * width, width)
+        fetch.append(pltpu.make_async_copy(we_in.at[:, cols], we.at[part], load.at[1 + 2 * part]))
+        fetch.append(pltpu.make_async_copy(wc_in.at[cols, :], wc.at[part], load.at[2 + 2 * part]))
+    for copy in fetch:
+        copy.start()
+
+    def keep(block):
+        return pltpu.make_async_copy(acts.at[block], acts_out.at[block], store.at[block])
+
+    gain = gain_ref[...].reshape(1, width)
+    low, up, attended, branch = 2 * parts, 2 * parts + 1, 2 * parts + 2, 2 * parts + 3
+    for row in range(micro):
+        at = slice(row * rows, (row + 1) * rows)
+        acts[attended, at, :] = columns_of(received, row, rows, blocks)
+        acts[up, at, :] = up_ref[row]
+    fetch[0].wait()
+    mixed[...] = dot_nn(acts[attended], wo[...])
+    for row in range(micro):
+        at = slice(row * rows, (row + 1) * rows)
+        mixed[at, :] += x_ref[row].astype(f32)
+        unit, _ = normal(mixed[at, :])
+        acts[low, at, :] = (unit * gain).astype(bf16)
+    result_acc[...] = mixed[...]
+    second_acc[...] = jnp.zeros_like(second_acc)
+    for block in (up, attended, low):
+        keep(block).start()
+
+    for part in range(parts):
+        fetch[1 + 2 * part].wait()
+        fetch[2 + 2 * part].wait()
+
+        @pl.loop(0, micro)
+        def _(row):
+            at = pl.ds(pl.multiple_of(row * rows, rows), rows)
+            hidden = dot_nn(acts[low, at, :], we[part])
+            active_grad = dot_nt(acts[up, at, :], wc[part])
+            square = hidden * hidden
+            c = 0.7978845608028654
+            bend = jnp.tanh(hidden * (c + 0.044715 * c * square))
+            gate = 0.5 + 0.5 * bend
+            slope = gate + 0.5 * hidden * (1.0 - bend * bend) * (c + 3.0 * 0.044715 * c * square)
+            active = (hidden * gate).astype(bf16)
+            grad = (active_grad * slope).astype(bf16)
+            acts[part, at, :] = active
+            acts[parts + part, at, :] = grad
+            result_acc[at, :] += dot_nn(active, wc[part])
+            second_acc[at, :] += dot_nt(grad, we[part])
+
+        keep(part).start()
+        keep(parts + part).start()
+
+    for row in range(micro):
+        at = slice(row * rows, (row + 1) * rows)
+        unit, scale = normal(mixed[at, :])
+        grad = acts[up, at, :].astype(f32) + normal_pull(second_acc[at, :] * gain, unit, scale)
+        mixed_grad_ref[row] = grad
+        acts[branch, at, :] = grad.astype(bf16)
+    keep(branch).start()
+    back = dot_nt(acts[branch], wo[...]).astype(bf16)
+    for row in range(micro):
+        at = slice(row * rows, (row + 1) * rows)
+        result_ref[row] = result_acc[at, :].astype(bf16)
+        for chip in range(chips):
+            start = chip * heads * HEAD
+            wide, narrow = pack_heads(
+                [back[at, start + h * HEAD : start + (h + 1) * HEAD] for h in range(heads)]
+            )
+            attended_grad_ref[2 * chip + row, :rows, :] = wide
+            attended_grad_ref[2 * chip + row, rows:, :] = narrow
+    for block in range(2 * parts + 4):
+        keep(block).wait()
+
+
+def final_kernel(
+    final, we_ref, unit_ref, first_gain, second_gain, wq_ref, wkv_ref,
+    first_ref, query_ref, pair_ref, output_ref, second_ref, expand_ref, contract_ref,
+    first_acc, second_acc,
+):
+    step = pl.program_id(0)
+    width = wq_ref.shape[0]
+    chips = unit_ref.shape[0]
+    heads = width // HEAD // chips
+    parts = (pl.num_programs(0) - 4) // 2
+
+    def fold(array):
+        return sum(array[:, i : i + LANES] for i in range(0, width, LANES))
+
+    @pl.when(step == 0)
+    def _():
+        first_acc[...] = jnp.zeros_like(first_acc)
+        second_acc[...] = jnp.zeros_like(second_acc)
+
+    @pl.when(step < parts)
+    def _():
+        contract_ref[...] = final[0].astype(f32)
+
+    @pl.when((step >= parts) & (step < 2 * parts))
+    def _():
+        value = final[0].astype(f32)
+        expand_ref[...] = value
+        second_acc[...] += fold(value * we_ref[...].astype(f32))
+
+    @pl.when(step == 2 * parts)
+    def _():
+        output_ref[...] = final[0].astype(f32)
+
+    def columns(place):
+        return jnp.concatenate(
+            [unit_ref[chip][:, place(head) : place(head) + HEAD] for chip in range(chips) for head in range(heads)], 1
+        ).astype(f32)
+
+    @pl.when(step == 2 * parts + 1)
+    def _():
+        value = columns(lambda head: heads * LANES + head * HEAD)
+        query_ref[...] = value
+        first_acc[...] += fold(value * wq_ref[...].astype(f32))
+
+    for side in range(2):
+
+        @pl.when(step == 2 * parts + 2 + side)
+        def _():
+            value = columns(lambda head: head * LANES + (HEAD if side == 0 else 0))
+            pair_ref[...] = value
+            first_acc[...] += fold(value * wkv_ref[:, side * width : (side + 1) * width].astype(f32))
+
+    @pl.when(step == pl.num_programs(0) - 1)
+    def _():
+        first_ref[...] = jnp.sum(jnp.transpose(first_acc[...]), 0) / first_gain[...]
+        second_ref[...] = jnp.sum(jnp.transpose(second_acc[...]), 0) / second_gain[...]
 
 
 VMEM = pl.BlockSpec(memory_space=pltpu.VMEM)
 SMEM = pl.BlockSpec(memory_space=pltpu.SMEM)
+ANY = pl.BlockSpec(memory_space=pl.ANY)
 
 
 def attention_forward(inputs, gain, lengths, views, padding, query_weight, pair_weight, blocks):
@@ -532,25 +1339,28 @@
     packed = rows * heads // 2
     shape = jax.ShapeDtypeStruct
     dma = pltpu.SemaphoreType.DMA
+    unit = (heads, total, LANES)
     return pl.pallas_call(
         forward_kernel,
         out_shape=(
-            shape((blocks, rows, width), bf16),
-            shape((heads, total, LANES), bf16),
-            shape((heads, total, LANES), bf16),
-            shape((heads, total, LANES), bf16),
-            shape((heads, total, LANES), f32),
+            shape((blocks // 2, 2 * rows, width), bf16),
+            shape(unit, bf16),
+            shape(unit, bf16),
+            shape(unit, bf16),
+            shape((blocks, packed, LANES), bf16),
             shape((blocks, packed, LANES), bf16),
         ),
         in_specs=[SMEM, SMEM] + [VMEM] * 5,
-        out_specs=(VMEM,) * 6,
+        out_specs=(ANY,) * 5 + (VMEM,),
         scratch_shapes=[
+            pltpu.VMEM((blocks, rows, width), bf16),
+            pltpu.VMEM(unit, bf16),
+            pltpu.VMEM(unit, bf16),
+            pltpu.VMEM(unit, bf16),
+            pltpu.VMEM(unit, f32),
             pltpu.VMEM((width, heads * 3 * LANES), bf16),
             pltpu.VMEM((rows, width), bf16),
-            pltpu.VMEM((blocks, heads, rows, rows), f32),
-            pltpu.VMEM((heads, rows, LANES), f32),
-            pltpu.VMEM((heads, rows, LANES), f32),
-            pltpu.VMEM((heads, rows, LANES), f32),
+            pltpu.VMEM(unit, f32),
             pltpu.VMEM((blocks, packed, LANES), bf16),
             dma,
             dma,
@@ -558,66 +1368,148 @@
             dma((blocks,)),
             dma((blocks,)),
             dma((blocks,)),
+            dma((blocks, 5)),
         ],
         compiler_params=pltpu.CompilerParams(
-            collective_id=0, has_side_effects=True, vmem_limit_bytes=60 << 20
+            collective_id=0, has_side_effects=True, vmem_limit_bytes=50 << 20
         ),
         name="attention_forward",
-    )(lengths, views, inputs, gain.reshape(1, width), padding.reshape(micro, blocks, rows), query_weight, pair_weight)
-
-
-def attention_backward(grad, normed, qa, ka, va, out):
-    micro, rows, width = grad.shape
-    blocks = normed.shape[0]
+    )(lengths, views, inputs, gain, padding, query_weight, pair_weight)
+
+
+def attention_backward(grad, mixed_grad, gain, acts, normed, qa, ka, va, out, query_weight, pair_weight, inputs):
+    micro, rows, width = inputs.shape
+    blocks, packed, _ = grad.shape
     heads, total, _ = qa.shape
-    packed = rows * heads // 2
+    chips = blocks // 2
+    pieces = acts.shape[0] - 3
+    count = 2 * pieces
+    unit_lanes = (heads + 2) * LANES
+    side = width // 2
     shape = jax.ShapeDtypeStruct
     dma = pltpu.SemaphoreType.DMA
+    unit = pltpu.VMEM((heads, total, LANES), bf16)
+    message = pltpu.VMEM((blocks, packed, LANES), bf16)
+    pair = pltpu.VMEM((blocks, heads * rows, LANES), bf16)
     return pl.pallas_call(
         backward_kernel,
         out_shape=(
-            shape((blocks, packed, LANES), bf16),
-            shape((blocks, heads * rows, LANES), bf16),
-            shape((width, (heads + 2) * LANES), f32),
+            shape(inputs.shape, bf16),
+            shape((pieces, width, width), bf16),
+            shape((chips, width, unit_lanes), bf16),
         ),
-        in_specs=[VMEM] * 6,
-        out_specs=(VMEM,) * 3,
+        in_specs=[VMEM] * 3 + [ANY] * 9,
+        out_specs=(VMEM, ANY, ANY),
         scratch_shapes=[
-            pltpu.VMEM((blocks, packed, LANES), bf16),
-            pltpu.VMEM((blocks, packed, LANES), bf16),
-            pltpu.VMEM((heads, total, LANES), bf16),
-            pltpu.VMEM((heads, total, LANES), f32),
-            pltpu.VMEM((heads, rows, LANES), f32),
-            pltpu.VMEM((heads, rows, LANES), f32),
-            pltpu.VMEM((heads + 2, total, LANES), bf16),
-            pltpu.VMEM((blocks, packed, LANES), bf16),
-            pltpu.VMEM((blocks, heads * rows, LANES), bf16),
-            dma((blocks,)),
-            dma((blocks,)),
-            dma((blocks,)),
-            dma((blocks,)),
-            dma((blocks,)),
-            dma((blocks,)),
-        ],
+            pltpu.VMEM(acts.shape, bf16),
+            unit,
+            unit,
+            unit,
+            message,
+            message,
+            unit,
+            unit,
+            pltpu.VMEM((heads, HEAD, total), bf16),
+            pltpu.VMEM((heads, HEAD, total), f32),
+            pltpu.VMEM((heads, 2 * rows, LANES), f32),
+            message,
+            pair,
+            message,
+            pair,
+            pltpu.VMEM((side, unit_lanes), f32),
+            pltpu.VMEM((GIVE, side, side), bf16),
+            dma((acts.shape[0],)),
+            dma((4,)),
+            dma((chips + 6 + micro,)),
+        ]
+        + [dma((blocks,))] * 6
+        + Sums.scratch(count, side, side)
+        + UnitSum.scratch(chips, side, unit_lanes),
         compiler_params=pltpu.CompilerParams(
-            collective_id=1, has_side_effects=True, vmem_limit_bytes=60 << 20
+            collective_id=1, has_side_effects=True, vmem_limit_bytes=62 << 20
         ),
         name="attention_backward",
-    )(grad, normed, qa, ka, va, out)
-
-
-def unpack_heads(packed, rows):
-    wide = packed[..., :rows, :]
-    narrow = packed[..., rows:, :]
-    third = jnp.concatenate([narrow[..., :HEAD], narrow[..., HEAD:]], -2)
-    return jnp.concatenate([wide, third], -1)
-
-
-def by_token(received, rows):
-    parts = unpack_heads(received, rows)
-    chips = parts.shape[0] // 2
-    parts = parts.reshape(chips, 2, rows, -1)
-    return jnp.transpose(parts, (1, 2, 0, 3)).reshape(2 * rows, -1)
+    )(grad, mixed_grad, gain, acts, normed, qa, ka, va, out, query_weight, pair_weight, inputs)
+
+
+def dense(received, inputs, cotangent, gain, output_weight, expand_weight, contract_weight):
+    micro, rows, width = inputs.shape
+    tokens = micro * rows
+    parts = expand_weight.shape[1] // width
+    shape = jax.ShapeDtypeStruct
+    dma = pltpu.SemaphoreType.DMA
+    acts = (2 * parts + 4, tokens, width)
+    return pl.pallas_call(
+        dense_kernel,
+        out_shape=(
+            shape((micro, rows, width), bf16),
+            shape((micro, rows, width), f32),
+            shape(received.shape, bf16),
+            shape(acts, bf16),
+        ),
+        in_specs=[VMEM] * 4 + [ANY] * 3,
+        out_specs=(VMEM,) * 3 + (ANY,),
+        scratch_shapes=[
+            pltpu.VMEM((width, width), bf16),
+            pltpu.VMEM((parts, width, width), bf16),
+            pltpu.VMEM((parts, width, width), bf16),
+            pltpu.VMEM(acts, bf16),
+            pltpu.VMEM((tokens, width), f32),
+            pltpu.VMEM((tokens, width), f32),
+            pltpu.VMEM((tokens, width), f32),
+            dma((1 + 2 * parts,)),
+            dma((acts[0],)),
+        ],
+        compiler_params=pltpu.CompilerParams(vmem_limit_bytes=56 << 20),
+        name="dense",
+    )(received, inputs, cotangent, gain, output_weight, expand_weight, contract_weight)
+
+
+def finish(final, unit_final, first_gain, second_gain, query_weight, pair_weight, expand_weight):
+    pieces, width, _ = final.shape
+    steps = pieces + 3
+    parts = (pieces - 1) // 2
+    shape = jax.ShapeDtypeStruct
+    square = (width, width)
+
+    def whole(array):
+        return pl.BlockSpec(array.shape, lambda p: (0,) * array.ndim)
+
+    def clip(p, start, count):
+        return jnp.clip(p - start, 0, count - 1)
+
+    fixed = (unit_final, first_gain, second_gain, query_weight, pair_weight)
+    row = pl.BlockSpec((width,), lambda p: (0,))
+    return pl.pallas_call(
+        final_kernel,
+        grid=(steps,),
+        out_shape=(
+            shape((width,), f32),
+            shape(square, f32),
+            shape((width, 2 * width), f32),
+            shape(square, f32),
+            shape((width,), f32),
+            shape((width, parts * width), f32),
+            shape((parts * width, width), f32),
+        ),
+        in_specs=[
+            pl.BlockSpec((1,) + square, lambda p: (clip(p, 0, pieces), 0, 0)),
+            pl.BlockSpec(square, lambda p: (0, clip(p, parts, parts))),
+        ]
+        + [whole(array) for array in fixed],
+        out_specs=(
+            row,
+            pl.BlockSpec(square, lambda p: (0, 0)),
+            pl.BlockSpec(square, lambda p: (0, clip(p, 2 * parts + 2, 2))),
+            pl.BlockSpec(square, lambda p: (0, 0)),
+            row,
+            pl.BlockSpec(square, lambda p: (0, clip(p, parts, parts))),
+            pl.BlockSpec(square, lambda p: (clip(p, 0, parts), 0)),
+        ),
+        scratch_shapes=[pltpu.VMEM((width, LANES), f32), pltpu.VMEM((width, LANES), f32)],
+        compiler_params=pltpu.CompilerParams(vmem_limit_bytes=56 << 20),
+        name="finish",
+    )(final, expand_weight, *fixed)
 
 
 def layer_norm(value, gain):
@@ -927,60 +1819,19 @@
     inputs, cotangent, lengths, view_counts, padding, first_gain, query_weight, key_value_weight,
     output_weight, second_gain, expand_weight, contract_weight,
 ):
-    micro, rows, width = inputs.shape
-    blocks = lax.axis_size("blk")
-    normed_all, qa, ka, va, out, received = attention_forward(
-        inputs, first_gain, lengths, view_counts, padding, query_weight, key_value_weight, blocks
+    normed, qa, ka, va, out, received = attention_forward(
+        inputs, first_gain, lengths, view_counts, padding, query_weight, key_value_weight, lax.axis_size("blk")
     )
-    gelu = partial(jax.nn.gelu, approximate=True)
-    flat = inputs.reshape(micro * rows, width).astype(f32)
-    upstream = cotangent.reshape(micro * rows, width)
-    _, first_pull = jax.vjp(layer_norm, flat, first_gain)
-    attended = by_token(received, rows)
-    mixed = flat + jnp.dot(attended, output_weight, preferred_element_type=f32)
-    second, second_pull = jax.vjp(layer_norm, mixed, second_gain)
-    second = second.astype(bf16)
-    hidden = jnp.dot(second, expand_weight, preferred_element_type=f32)
-    activated, gelu_pull = jax.vjp(gelu, hidden)
-    activated = activated.astype(bf16)
-    result = (mixed + jnp.dot(activated, contract_weight, preferred_element_type=f32)).astype(bf16)
-    hidden_grad = gelu_pull(dot_nt(upstream, contract_weight))[0].astype(bf16)
-    second_grad = dot_nt(hidden_grad, expand_weight)
-    mixed_part, grad_second = second_pull(second_grad)
-    mixed_grad = upstream.astype(f32) + mixed_part
-    branch_grad = mixed_grad.astype(bf16)
-    attended_grad = dot_nt(branch_grad, output_weight).astype(bf16)
-    grad_contract = dot_tn(activated, upstream)
-    grad_expand = dot_tn(second, hidden_grad)
-    grad_output = dot_tn(attended, branch_grad)
-    got_query, got_pair, unit_grad = attention_backward(
-        attended_grad.reshape(micro, rows, width), normed_all, qa, ka, va, out
+    result, mixed_grad, attended_grad, acts = dense(
+        received, inputs, cotangent, second_gain, output_weight, expand_weight, contract_weight
     )
-    heads = qa.shape[0]
-    chips = blocks // 2
-    query_grad = by_token(got_query, rows)
-    pair_grad = got_pair.reshape(chips, 2, heads, rows, 2, HEAD)
-    pair_grad = jnp.transpose(pair_grad, (1, 3, 4, 0, 2, 5)).reshape(micro * rows, 2 * width)
-    normed_grad = dot_nt(query_grad, query_weight) + dot_nt(pair_grad, key_value_weight)
-    input_part, grad_first = first_pull(normed_grad)
-    input_grad = (mixed_grad + input_part).astype(bf16)
-    z = lax.axis_index("blk") // 2
-    pair_part = unit_grad[:, : heads * LANES].reshape(width, heads, 2, HEAD)
-    pair_part = jnp.transpose(pair_part, (0, 2, 1, 3)).reshape(width, 2, heads * HEAD)
-    query_part = unit_grad[:, heads * LANES : heads * LANES + heads * HEAD]
-    grad_pair = lax.dynamic_update_slice(
-        jnp.zeros((width, 2, width), f32), pair_part, (0, 0, z * heads * HEAD)
-    ).reshape(width, 2 * width)
-    grad_query = lax.dynamic_update_slice(
-        jnp.zeros((width, width), f32), query_part, (0, z * heads * HEAD)
+    input_grad, final, unit_final = attention_backward(
+        attended_grad, mixed_grad, first_gain, acts, normed, qa, ka, va, out, query_weight, key_value_weight, inputs
     )
-    wide = [g.astype(bf16) for g in (grad_query, grad_pair, grad_output, grad_expand, grad_contract)]
-    wide = [g.astype(f32) for g in lax.psum(tuple(wide), ("dp", "blk"))]
-    gains = lax.psum((grad_first, grad_second), ("dp", "blk"))
-    return (
-        result.reshape(micro, rows, width), input_grad.reshape(micro, rows, width),
-        gains[0], wide[0], wide[1], wide[2], gains[1], wide[3], wide[4],
+    first, query, pair, output, second, expand, contract = finish(
+        final, unit_final, first_gain, second_gain, query_weight, key_value_weight, expand_weight
     )
+    return result, input_grad, first, query, pair, output, second, expand, contract
 
 
 def solution(mesh):

time: 680 us -> 299 us (0.44)
  waiting for transfers between devices: 179 us -> 0 us
  blocking collectives: 150 us -> 0 us
  Pallas kernels: 190 us -> 288 us
  local copies, waits for them, and re-layouts: 70.3 us -> 7.8 us
  matrix products: 45.4 us -> 0 us
  other arithmetic: 23.3 us -> 0 us
  between operations: 14.8 us -> 0.7 us
    psum x1 -> x0, waiting for transfers between devices: 179 us -> none  [fast_on_device(): wide = [g.astype(f32) for g in lax.psum(tuple(wide), ('dp', 'blk'))]]
    psum x1 -> x0, blocking collectives: 150 us -> none  [fast_on_device(): gains = lax.psum((grad_first, grad_second), ('dp', 'blk'))]
    pallas_call x2 -> x4, Pallas kernels: 190 us -> 288 us  [the longest x1 156 us: attention_backward(): pl.pallas_call(backward_kernel, out_shape=(shape(inputs.shape, bf16), sha...]
    dot_general x11 -> x0, matrix products: 45.4 us -> none  [the longest x3 14.9 us: dot_tn(): lax.dot_general(a, b, (((0,), (0,)), ((), ())), preferred_element_type=f32)]
    dynamic_update_slice x2 -> x0, local copies, waits for them, and re-layouts: 36.4 us -> none  [the longest x1 32.5 us: fast_on_device(): lax.dynamic_update_slice(jnp.zeros((width, 2, width), f32), pair_part, (0...]
    convert_element_type x7 -> x0, other arithmetic: 20.5 us -> none  [the longest x5 17.1 us: fast_on_device(): wide = [g.astype(f32) for g in lax.psum(tuple(wide), ('dp', 'blk'))]]
    reshape x5 -> x0, local copies, waits for them, and re-layouts: 6.82 us -> none  [the longest x2 2.73 us: by_token(): parts = parts.reshape(chips, 2, rows, -1)]
    unnamed x53 -> x19, local copies, waits for them, and re-layouts: 13.9 us -> 7.8 us
  transfers between devices with their start and end apart: 1 -> 0, of which waited for: 1 -> 0; matrix products, arithmetic and copies ran while one was open for 4% -> 0% of each run, Pallas kernels for 0% -> 0%
where the time goes in v2:
time: 299 us; the launch traced here: 296 us
  Pallas kernels  288 us (96%)
  local copies, waits for them, and re-layouts  7.8 us (3%)
    pallas_call x1, Pallas kernels, attention_backward(): pl.pallas_call(backward_kernel, out_shape=(shape(inputs.shape, bf16), sha...  156 us
    pallas_call x1, Pallas kernels, attention_forward(): pl.pallas_call(forward_kernel, out_shape=(shape((blocks // 2, 2 * rows, w...  90.7 us
    pallas_call x1, Pallas kernels, finish(): pl.pallas_call(final_kernel, grid=(steps,), out_shape=(shape((width,), f3...  21.8 us
    pallas_call x1, Pallas kernels, dense(): pl.pallas_call(dense_kernel, out_shape=(shape((micro, rows, width), bf16)...  19.7 us
    unnamed x19, local copies, waits for them, and re-layouts  7.8 us

profile of v2, /device:TPU:0, one launch (start us, length us, event | category | flops | bytes accessed | tf_op | source)
XLA Modules:
  0.0 296.2 jit_solution(13726489190331433921)
XLA Ops:
  0.6 0.0 copy-start
  0.7 1.3 copy-done
  1.9 0.0 copy-start.1
  1.9 1.1 copy-done.1
  3.0 0.0 copy-start.4
  3.1 0.7 copy-done.4
  3.7 0.0 copy-start.5
  3.7 0.7 copy-done.5
  4.5 0.0 copy-start.6
  4.5 0.7 copy-done.6
  5.1 0.0 copy-start.7
  5.1 0.7 copy-done.7
  5.8 90.7 %attention_forward.1 = (bf16[4,512,768]{2,1,0:T(8,128)(2,1)}, bf16[3,2048,128]{2,1,0:T(8,128)(2,1)}, bf16[3,2048,128]{2,1,0:T(8,128)(2,1)}, bf16[3,2048,128]{2,1...) custom-call(s32[2,4]{1,0:T(2,128)S(1)} %copy-done.6, s32[2,4]{1,0:T(2,128)S(1)} %copy-done.7, ...), custom_call_target="tpu_custom_call" | custom-call | tf_op jit(solution)/shard_map/attention_forward/pallas_call | solution.py:1343
  96.5 0.0 copy-start.2
  96.6 0.9 copy-done.2
  97.4 0.0 copy-start.3
  97.4 0.9 copy-done.3
  98.3 19.7 %dense.1 = (bf16[2,256,768]{2,1,0:T(8,128)(2,1)}, f32[2,256,768]{2,1,0:T(8,128)}, bf16[8,384,128]{2,1,0:T(8,128)(2,1)}, bf16[12,512,768]{2,1,0:T(8,128)(2,1)}) custom-call(bf16[8,384,128]{2,1,0:T(8,128)(2,1)} %copy-done.3, bf16[2,256,768]{2,1,0:T(8,128)(2,1)} %x_in.1, bf16[2,256,768]{2,1,0:T(8,128)(2,1)} %up_ref.1, f32[768]{0:T(1024)} %second_gain.1, ...), custom_call_target="tpu_custom_call" | custom-call | tf_op jit(solution)/shard_map/dense/pallas_call | solution.py:1442
  118.0 155.5 %attention_backward.1 = (bf16[2,256,768]{2,1,0:T(8,128)(2,1)}, bf16[9,768,768]{2,1,0:T(8,128)(2,1)}, bf16[4,768,640]{2,1,0:T(8,128)(2,1)}) custom-call(bf16[8,384,128]{2,1,0:T(8,128)(2,1)} %get-tuple-element.31.grad_ref, f32[2,256,768]{2,1,0:T(8,128)} %get-tuple-element.32.mixed_grad_ref, f32[768]{0:T(1024)} %first_gain.1, ...), custom_call_target="tpu_custom_call" | custom-call | tf_op jit(solution)/shard_map/attention_backward/pallas_call | solution.py:1394
  273.5 0.0 copy-start.8
  273.5 21.8 %finish.1 = (f32[768]{0:T(1024)}, f32[768,768]{1,0:T(8,128)}, f32[768,1536]{1,0:T(8,128)}, f32[768,768]{1,0:T(8,128)}, f32[768]{0:T(1024)}, /*index=5*/f32[768,3072]{1,0:T(8,128)}, f32[3072,768]{1,0:T(8,128)}) custom-call(bf16[9,768,768]{2,1,0:T(8,128)(2,1)} %get-tuple-element.40.final, bf16[768,3072]{1,0:T(8,128)(2,1)} %we_ref.1, ...), custom_call_target="tpu_custom_call" | custom-call | tf_op jit(solution)/shard_map/finish/pallas_call | solution.py:1483
  295.3 0.0 copy-done.8
  295.3 0.9 copy.22
Async XLA Ops:
  0.6 1.3 copy-start
  1.9 1.1 copy-start.1
  3.0 0.7 copy-start.4
  3.7 0.7 copy-start.5
  4.5 0.7 copy-start.6
  5.1 0.7 copy-start.7
  96.5 0.9 copy-start.2
  97.4 0.9 copy-start.3
  273.5 21.8 %copy-start.8 = (bf16[2,256,768]{2,1,0:T(8,128)(2,1)S(1)}, bf16[2,256,768]{2,1,0:T(8,128)(2,1)}, u32[]{:S(2)}) copy-start(bf16[2,256,768]{2,1,0:T(8,128)(2,1)} %get-tuple-element.59) | copy-start | bytes 2359300

commit v3 on v2

--- a/solution.py
+++ b/solution.py
@@ -11,14 +11,16 @@
 PATCHES = 64
 CODES = 40
 BIG = 1e30
-EARLY = 6
+EARLY = 12
 OUT_AT = (0, 3, 6, 9, 12)
 BACK_AT = (0, 3, 6, 9)
 LATE = 13
-GIVE = 4
-PAIR_SLOTS = (10, 14, 18, 21, 23, 24, 22)
-QUERY_SLOTS = (25, 27, 29, 31, 33, 34, 27)
-UNIT_SLOTS = (1, 3, 5, 8, 11, 14, 16)
+GIVE = 3
+PAIR_SLOTS = (18, 23, 28, 31, 34, 35, 28)
+QUERY_SLOTS = (36, 37, 38, 39, 40, 40, 31)
+PAIR_SUM_SLOTS = (0, 2, 4, 6, 9, 11, 14)
+QUERY_SUM_SLOTS = (1, 3, 5, 8, 10, 12, 15)
+PAIR_DONE = 40
 OUT = (1, 2, 3, 4, 5)
 BACK = (6, 7, 8, 9)
 LANES = 128
@@ -155,10 +157,10 @@
 
 
 def forward_kernel(
-    lengths, views, x_ref, gain_ref, pad_ref, wq_ref, wkv_ref,
+    lengths, views, x_ref, gain_ref, pad_ref, wq_in, wkv_in,
     normed_out, qa_out, ka_out, va_out, o_out, received,
-    normed, qa, ka, va, o_ref, weight, stage, peak, outgoing,
-    sib_send, sib_recv, line_send, line_recv, out_send, out_recv, store,
+    normed, qa, ka, va, o_ref, weight, wq_ref, wkv_ref, stage, peak, outgoing,
+    fetch, sib_send, sib_recv, line_send, line_recv, out_send, out_recv, store,
 ):
     rows, width = x_ref.shape[1], x_ref.shape[2]
     blocks = normed.shape[0]
@@ -171,6 +173,12 @@
     lane = lax.broadcasted_iota(jnp.int32, (rows, LANES), 1)
 
     arrived = greet(dp, me, blocks)
+    loads = [
+        pltpu.make_async_copy(wq_in, wq_ref, fetch.at[0]),
+        pltpu.make_async_copy(wkv_in, wkv_ref, fetch.at[1]),
+    ]
+    for copy in loads:
+        copy.start()
     gain = gain_ref[...].reshape(1, width)
 
     def norm(value):
@@ -222,6 +230,8 @@
     )
     sib_copy.start()
 
+    for copy in loads:
+        copy.wait()
     gap = jnp.zeros((width, LANES - HEAD), bf16)
     for chip in range(blocks // 2):
 
@@ -820,51 +830,107 @@
 
 
 def backward_kernel(
-    grad_ref, mixed_grad_ref, gain_ref, acts_in, normed_in, qa_in, ka_in, va_in, o_in, wq_in, wkv_in, x_in,
-    input_grad, final, unit_final,
-    acts, qa, ka, va, out, received, doa, right_key, key_turned, dqt, dvk, send_query, send_pair,
-    got_query, got_pair, unit, give,
-    load_acts, load_heads, load_late, out_send, out_recv, query_send, query_recv, pair_send, pair_recv,
-    *sum_refs,
+    first_gain, second_gain, received_in, x_in, up_in, normed_in, qa_in, ka_in, va_in, o_in,
+    wq_in, wkv_in, wo_in, we_in, wc_in,
+    result_ref, input_grad, final, pair_final, query_final,
+    acts, pool, result_acc, second_acc, out, grad_out, received, key_turned, dqt, dvk, send_query, send_pair,
+    got_query, give,
+    load_tiles, load_first, load_heads, load_late, out_send, out_recv, query_send, query_recv, pair_send, pair_recv,
+    save, *sum_refs,
 ):
-    blocks, packed = grad_ref.shape[0], grad_ref.shape[1]
+    blocks, packed = grad_out.shape[0], grad_out.shape[1]
     rows = 2 * packed // 3
     micro, _, width = input_grad.shape
-    heads = qa.shape[0]
+    heads, _, total = key_turned.shape
     chips = blocks // 2
+    tall = acts.shape[1]
+    tiles = width // LANES
     dp = lax.axis_index("dp")
     me = lax.axis_index("blk")
     z = me // 2
     core = lax.rem(me, 2)
     lane = lax.broadcasted_iota(jnp.int32, (rows, LANES), 1)
     sums = Sums.gather(final, sum_refs[:26])
-    units = UnitSum(sums, unit_final, sum_refs[26:])
+    pair_sum = UnitSum(sums, pair_final, sum_refs[26:41])
+    query_sum = UnitSum(sums, query_final, sum_refs[41:])
     count = sums.count
+    parts = (count // 2 - 1) // 2
+    low, up, attended, branch = 2 * parts, 2 * parts + 1, 2 * parts + 2, 2 * parts + 3
     arrived = greet(dp, me, blocks, (sums.along_x, sums.along_y))
 
-    def load(block):
-        return pltpu.make_async_copy(acts_in.at[block], acts.at[block], load_acts.at[block])
+    at_query, at_key, at_value, at_grad, at_right, at_pair = (number * heads * total for number in range(6))
+
+    def in_pool(base, head, start, size):
+        return pl.ds(pl.multiple_of(base + head * total + start, LANES), size)
+
+    def pair_rows(block):
+        size = heads * rows
+        return pl.ds(pl.multiple_of(at_pair + block * size, size), size)
+
+    def fetch(number):
+        part = number % parts
+        copies = []
+        for tile in range(tiles):
+            if number < parts:
+                src = we_in.at[:, pl.ds(part * width + tile * LANES, LANES)]
+            else:
+                src = wc_in.at[pl.ds(part * width, width), pl.ds(tile * LANES, LANES)]
+            place = number * tiles + tile
+            copies.append(
+                pltpu.make_async_copy(src, pool.at[pl.ds(place * width, width)], load_tiles.at[place])
+            )
+        return copies
+
+    def weight(number):
+        return jnp.concatenate(
+            [pool[(number * tiles + tile) * width : (number * tiles + tile + 1) * width, :] for tile in range(tiles)], 1
+        )
+
+    def fetch_output():
+        return [
+            pltpu.make_async_copy(
+                wo_in.at[:, pl.ds(tile * LANES, LANES)], pool.at[pl.ds(tile * width, width)], load_tiles.at[tile]
+            )
+            for tile in range(tiles)
+        ]
+
+    def openers():
+        copies = [
+            pltpu.make_async_copy(received_in, send_query, load_first.at[0]),
+            pltpu.make_async_copy(wo_in.at[pl.ds(0, tall)], acts.at[parts], load_first.at[1]),
+            pltpu.make_async_copy(
+                wo_in.at[pl.ds(tall, width - tall)], acts.at[parts + 1, pl.ds(0, width - tall)], load_first.at[2]
+            ),
+        ]
+        for row in range(micro):
+            here = pl.ds(row * rows, rows)
+            copies.append(pltpu.make_async_copy(x_in.at[row], acts.at[branch, here], load_first.at[3 + 2 * row]))
+            copies.append(pltpu.make_async_copy(up_in.at[row], acts.at[up, here], load_first.at[4 + 2 * row]))
+        return copies
 
     def load_head(number):
         src = (qa_in, ka_in, va_in, o_in)[number]
-        return pltpu.make_async_copy(src, (qa, ka, va, out)[number], load_heads.at[number])
-
-    order = [9, 0, 1, 2, 3, 8, 4, 5, 6, 7, 10, 11]
-    for block in order[:3]:
-        load(block).start()
-    arrived()
+        base = (at_query, at_key, at_value)
+        dst = out if number == 3 else pool.at[pl.ds(base[number], heads * total)]
+        return pltpu.make_async_copy(src, dst, load_heads.at[number])
+
+    for copy in openers():
+        copy.start()
+    for part in range(parts):
+        for copy in fetch(part) + fetch(parts + part):
+            copy.start()
 
     kinds = {
-        "grad": (grad_ref, received, out_send, out_recv),
+        "grad": (grad_out, received, out_send, out_recv),
         "query": (send_query, got_query, query_send, query_recv),
-        "pair": (send_pair, got_pair, pair_send, pair_recv),
+        "pair": (send_pair, pool, pair_send, pair_recv),
     }
 
     def send(kind, block):
         src, dst, send_sem, recv_sem = kinds[kind]
         return pltpu.make_async_remote_copy(
             src_ref=src.at[block],
-            dst_ref=dst.at[me],
+            dst_ref=dst.at[pair_rows(me) if kind == "pair" else me],
             send_sem=send_sem.at[block],
             recv_sem=recv_sem.at[me],
             device_id=(dp, block),
@@ -875,27 +941,13 @@
         src, dst, send_sem, recv_sem = kinds[kind]
         return pltpu.make_async_remote_copy(
             src_ref=src.at[block],
-            dst_ref=dst.at[block],
+            dst_ref=dst.at[pair_rows(block) if kind == "pair" else block],
             send_sem=send_sem.at[block],
             recv_sem=recv_sem.at[block],
             device_id=(dp, block),
             device_id_type=MESH,
         )
 
-    for step in range(4):
-        for row in range(2):
-            block = 2 * far_order(z, jnp.int32(step)) + row
-
-            @pl.when(block != me)
-            def _():
-                send("grad", block).start()
-
-    for block in order[3:]:
-        load(block).start()
-    for number in range(4):
-        load_head(number).start()
-    received[me] = grad_ref[me]
-
     def message(number):
         return 2 * far_order(z, number // 2) + lax.rem(core + number, 2)
 
@@ -911,44 +963,118 @@
         sums.tick(OUT, OUT_AT, time, count)
         sums.tick(BACK, BACK_AT, time - LATE, count)
 
-    parts = (count // 2 - 1) // 2
     side = sums.half
 
     def weigh(piece):
         whole = piece // 2
-        left = jnp.where(whole < parts, whole, jnp.where(whole < 2 * parts, 2 * parts, 2 * parts + 2))
-        right = jnp.where(whole < parts, 2 * parts + 1, jnp.where(whole < 2 * parts, whole, 2 * parts + 3))
+        left = jnp.where(whole < parts, whole, jnp.where(whole < 2 * parts, low, attended))
+        right = jnp.where(whole < parts, up, jnp.where(whole < 2 * parts, whole, branch))
         cols = pl.ds(pl.multiple_of(lax.rem(piece, 2) * side, LANES), side)
         turn = lax.rem(piece, GIVE)
 
+        theirs = pl.ds(pl.multiple_of((1 - core) * side, 16), side)
+        ours = pl.ds(pl.multiple_of(core * side, 16), side)
+
         @pl.when(piece >= GIVE)
         def _():
-            sums.to_core(piece - GIVE, give.at[turn]).wait_send()
-
-        operand = acts[right, :, cols]
-        theirs = pl.ds(pl.multiple_of((1 - core) * side, LANES), side)
-        give[turn] = dot_tn(acts[left, :, theirs], operand).astype(bf16)
-        sums.to_core(piece, give.at[turn]).start()
-        ours = pl.ds(pl.multiple_of(core * side, LANES), side)
-        sums.own[piece] = dot_tn(acts[left, :, ours], operand).astype(bf16)
-
-    per_slot = count // EARLY
-    for number in range(EARLY):
-        if number == 0:
-            for block in order[:5]:
-                load(block).wait()
-        if number == 2:
-            for block in order[5:]:
-                load(block).wait()
-
-        @pl.loop(0, per_slot)
+            sums.to_core(piece - GIVE, give.at[turn, theirs]).wait_send()
+
+        give[turn] = dot_tn(acts[left], acts[right, :, cols]).astype(bf16)
+        sums.to_core(piece, give.at[turn, theirs]).start()
+        sums.own[piece] = give[turn, ours, :]
+
+    opening = openers()
+    gain = second_gain[...].reshape(1, width)
+    opening[0].wait()
+    for row in range(micro):
+        acts[attended, row * rows : (row + 1) * rows, :] = columns_of(send_query, row, rows, blocks)
+    for copy in opening[1:]:
+        copy.wait()
+    for row in range(micro):
+        at = slice(row * rows, (row + 1) * rows)
+        value = acts[branch, at, :].astype(f32) + dot_nn(acts[attended, at, :tall], acts[parts])
+        value += dot_nn(acts[attended, at, tall:], acts[parts + 1, : width - tall])
+        result_acc[at, :] = value
+        acts[low, at, :] = (normal(value)[0] * gain).astype(bf16)
+    second_acc[...] = jnp.zeros_like(second_acc)
+
+    for part in range(parts):
+        for copy in fetch(part) + fetch(parts + part):
+            copy.wait()
+
+        @pl.loop(0, micro)
+        def _(row):
+            at = pl.ds(pl.multiple_of(row * rows, rows), rows)
+            widen, narrow = weight(part), weight(parts + part)
+            hidden = dot_nn(acts[low, at, :], widen)
+            active_grad = dot_nt(acts[up, at, :], narrow)
+            square = hidden * hidden
+            c = 0.7978845608028654
+            bend = jnp.tanh(hidden * (c + 0.044715 * c * square))
+            gate = 0.5 + 0.5 * bend
+            slope = gate + 0.5 * hidden * (1.0 - bend * bend) * (c + 3.0 * 0.044715 * c * square)
+            active = (hidden * gate).astype(bf16)
+            grad = (active_grad * slope).astype(bf16)
+            acts[part, at, :] = active
+            acts[parts + part, at, :] = grad
+            result_acc[at, :] += dot_nn(active, narrow)
+            second_acc[at, :] += dot_nt(grad, widen)
+
+        if part == 0:
+            arrived()
+            for copy in fetch_output():
+                copy.start()
+
+        @pl.loop(0, 2)
         def _(turn):
-            weigh(number * per_slot + turn)
-
+            weigh(2 * part + turn)
+            if part > 0:
+                slot(2 * part - 2 + turn)
+
+    for copy in fetch_output():
+        copy.wait()
+    project = weight(0)
+    for row in range(micro):
+        at = slice(row * rows, (row + 1) * rows)
+        result_ref[row] = result_acc[at, :].astype(bf16)
+        value = acts[branch, at, :].astype(f32) + dot_nn(acts[attended, at, :], project)
+        unit_, scale = normal(value)
+        grad = acts[up, at, :].astype(f32) + normal_pull(second_acc[at, :] * gain, unit_, scale)
+        second_acc[at, :] = grad
+        acts[branch, at, :] = grad.astype(bf16)
+        back = dot_nt(acts[branch, at, :], project).astype(bf16)
+        for chip in range(chips):
+            start = chip * heads * HEAD
+            wide, narrow = pack_heads(
+                [back[:, start + h * HEAD : start + (h + 1) * HEAD] for h in range(heads)]
+            )
+            grad_out[2 * chip + row, :rows, :] = wide
+            grad_out[2 * chip + row, rows:, :] = narrow
+
+    for step in range(4):
+        for row in range(2):
+            block = 2 * far_order(z, jnp.int32(step)) + row
+
+            @pl.when(block != me)
+            def _():
+                send("grad", block).start()
+
+    received[me] = grad_out[me]
+    for number in range(4):
+        load_head(number).start()
+
+    for number in range(2 * parts - 2, 2 * parts):
         slot(jnp.int32(number))
 
+    @pl.loop(2 * parts, count)
+    def _(piece):
+        weigh(piece)
+
+        @pl.when((lax.rem(piece, 2) == 1) & (piece > 2 * parts + 1))
+        def _():
+            slot(2 * parts + (piece - 2 * parts - 3) // 2)
+
     squares = [(wq_in, 0), (wkv_in, 0), (wkv_in, width)]
-    tall = acts.shape[1]
 
     def late():
         copies = [
@@ -989,10 +1115,10 @@
     def _(block):
         here = pl.ds(pl.multiple_of(block * rows, rows), rows)
         for head in range(heads):
-            key = ka[head, here, :][:, :HEAD].astype(f32)
+            key = pool[in_pool(at_key, head, block * rows, rows), :][:, :HEAD].astype(f32)
             key_turned[head, :, here] = jnp.transpose(key).astype(bf16)
-            query = qa[head, here, :][:, :HEAD]
-            right_key[head, here, :] = jnp.concatenate([jnp.zeros_like(query), query], 1)
+            query = pool[in_pool(at_query, head, block * rows, rows), :][:, :HEAD]
+            pool[in_pool(at_right, head, block * rows, rows), :] = jnp.concatenate([jnp.zeros_like(query), query], 1)
 
     @pl.loop(0, blocks)
     def _(step):
@@ -1002,7 +1128,6 @@
         def _():
             arrive("grad", block).wait_recv()
 
-        here = pl.ds(pl.multiple_of(block * rows, rows), rows)
         wide = received[block, :rows, :].astype(f32)
         narrow = received[block, rows:, :].astype(f32)
         shares = heads_of(wide * out[block, :rows, :].astype(f32), narrow * out[block, rows:, :].astype(f32))
@@ -1010,7 +1135,7 @@
         for head, piece in enumerate(heads_of(wide, narrow)):
             delta = jnp.sum(shares[head], -1, keepdims=True)
             value = jnp.concatenate([piece, gap], 1)
-            doa[head, here, :] = (value + spread(delta, HEAD, lane)).astype(bf16)
+            pool[in_pool(at_grad, head, block * rows, rows), :] = (value + spread(delta, HEAD, lane)).astype(bf16)
 
     wide_rows = 2 * rows
     eye = lax.broadcasted_iota(jnp.int32, (wide_rows, wide_rows), 0) == lax.broadcasted_iota(
@@ -1021,28 +1146,30 @@
     def pull(keys, queries, diagonal=False):
         found = []
         for head in range(heads):
-            k = ka[head, keys, :]
-            q = qa[head, queries, :]
-            g = doa[head, queries, :]
+            k = pool[in_pool(at_key, head, *keys), :]
+            q = pool[in_pool(at_query, head, *queries), :]
+            g = pool[in_pool(at_grad, head, *queries), :]
             at = lax.broadcasted_iota(jnp.int32, k.shape, 1)
             s = dot_nt(k, q)
             if diagonal:
                 bare = (at < HEAD) | (at > HEAD + CODES)
                 s = jnp.where(eye, dot_nt(jnp.where(bare, k, 0.0).astype(bf16), q), s)
             p = jnp.exp(s)
-            ds = (p * dot_nt(va[head, keys, :], g)).astype(bf16)
+            ds = (p * dot_nt(pool[in_pool(at_value, head, *keys), :], g)).astype(bf16)
             left = jnp.concatenate([p.astype(bf16), ds], 1)
             at = lax.broadcasted_iota(jnp.int32, g.shape, 1)
             value = jnp.where(at < HEAD, g, 0.0).astype(bf16)
-            right = jnp.concatenate([value, right_key[head, queries, :]], 0)
-            found.append((dot_nn(left, right), dot_nn(key_turned[head, :, keys], ds)))
+            right = jnp.concatenate([value, pool[in_pool(at_right, head, *queries), :]], 0)
+            turned = key_turned[head, :, pl.ds(pl.multiple_of(keys[0], LANES), keys[1])]
+            found.append((dot_nn(left, right), dot_nn(turned, ds)))
         return found
 
     @pl.loop(0, chips)
     def _(step):
         chip = far_order(z, step)
+        span = (chip * wide_rows, wide_rows)
         here = pl.ds(pl.multiple_of(chip * wide_rows, wide_rows), wide_rows)
-        for head, (pair, query) in enumerate(pull(here, here, True)):
+        for head, (pair, query) in enumerate(pull(span, span, True)):
             dvk[head] = pair
             dqt[head, :, here] += query
         time = EARLY
@@ -1055,7 +1182,7 @@
         @pl.loop(chip + 1, chips)
         def _(other):
             there = pl.ds(pl.multiple_of(other * wide_rows, wide_rows), wide_rows)
-            for head, (pair, query) in enumerate(pull(here, there)):
+            for head, (pair, query) in enumerate(pull(span, (other * wide_rows, wide_rows))):
                 dvk[head] += pair
                 dqt[head, :, there] += query
             slot(time + other - chip)
@@ -1063,9 +1190,8 @@
         @pl.when(chip > 0)
         def _():
             edge = chip * wide_rows
-            keys = pl.ds(pl.multiple_of(edge, half), half)
             queries = pl.ds(pl.multiple_of(edge - half, half), half)
-            for head, (pair, query) in enumerate(pull(keys, queries)):
+            for head, (pair, query) in enumerate(pull((edge, half), (edge - half, half))):
                 dvk[head, :half] += pair
                 dqt[head, :, queries] += query
             slot(time + chips - chip)
@@ -1079,11 +1205,28 @@
 
             @pl.when(block == me)
             def _():
-                got_pair[me] = send_pair[me]
+                pool[pair_rows(me), :] = send_pair[me]
+
+    for copy in late():
+        copy.wait()
+
+    def columns(tile):
+        right = jnp.concatenate([jnp.concatenate(tile(block), 1) for block in range(blocks)], 0)
+        for unit, which in (("give", 1 - core), ("own", core)):
+            cols = pl.ds(pl.multiple_of(which * side, LANES), side)
+            left = acts[:chips, :, cols].reshape(total, side)
+            yield unit, dot_tn(left, right).astype(bf16)
+
+    for unit, value in columns(
+        lambda block: [send_pair[block, head * rows : (head + 1) * rows, :] for head in range(heads)]
+    ):
+        getattr(pair_sum, unit)[...] = value
+        if unit == "give":
+            pair_sum.step(0)
+    slot(jnp.int32(EARLY + 13))
 
     @pl.loop(0, blocks)
-    def _(step):
-        block = step
+    def _(block):
         here = pl.ds(pl.multiple_of(block * rows, rows), rows)
         wide, narrow = pack_heads(
             [(jnp.transpose(dqt[h, :, here]) * (HEAD**-0.5)).astype(bf16) for h in range(heads)]
@@ -1095,196 +1238,120 @@
         def _():
             got_query[me] = send_query[me]
 
-    for copy in late():
-        copy.wait()
-
-    for turn in range(2):
-        which = 1 - core if turn == 0 else core
-        cols = pl.ds(pl.multiple_of(which * side, LANES), side)
-        unit[...] = jnp.zeros_like(unit)
-
-        @pl.loop(0, chips)
-        def _(chip):
-            tiles = []
-            for block in (2 * chip, 2 * chip + 1):
-                query = heads_of(send_query[block, :rows, :], send_query[block, rows:, :])
-                tile = [send_pair[block, head * rows : (head + 1) * rows, :] for head in range(heads)]
-                tile += query + [jnp.zeros((rows, LANES - HEAD), bf16)]
-                tiles.append(jnp.concatenate(tile, 1))
-            unit[...] += dot_tn(acts[chip, :, cols], jnp.concatenate(tiles, 0))
-
-        if turn == 0:
-            units.give[...] = unit[...].astype(bf16)
-            units.step(0)
-        else:
-            units.own[...] = unit[...].astype(bf16)
-        slot(jnp.int32(EARLY + 13 + turn))
+    gap = jnp.zeros((rows, LANES - HEAD), bf16)
+    for unit, value in columns(
+        lambda block: heads_of(send_query[block, :rows, :], send_query[block, rows:, :]) + [gap]
+    ):
+        getattr(query_sum, unit)[...] = value
+        if unit == "give":
+            query_sum.step(0)
+    slot(jnp.int32(EARLY + 14))
 
     ready = EARLY + 15
     end = LATE + count + BACK_AT[-1]
-    spots = [int(ready + place) for place in UNIT_SLOTS]
-
-    def last(row):
-        query = columns_of(got_query, row, rows, blocks)
+
+    def normed_part(row, operands, first):
+        grad = []
+        for part in range(2):
+            height = tall if part == 0 else width - tall
+            total_ = jnp.zeros((rows, height), f32)
+            for number, operand in enumerate(operands):
+                total_ = total_ + dot_nt(operand, acts[chips + 2 * (first + number) + part, :height])
+            grad.append(total_)
+        return jnp.concatenate(grad, 1)
+
+    def pair_part(row):
         keys, values = [], []
         for chip in range(chips):
             for head in range(heads):
-                both = got_pair[2 * chip + row, head * rows : (head + 1) * rows, :]
+                start = at_pair + ((2 * chip + row) * heads + head) * rows
+                both = pool[start : start + rows, :]
                 keys.append(both[:, HEAD:])
                 values.append(both[:, :HEAD])
-        grad = []
-        for part in range(2):
-            height = tall if part == 0 else width - tall
-            total = jnp.zeros((rows, height), f32)
-            for number, operand in enumerate(
-                (query, jnp.concatenate(keys, 1), jnp.concatenate(values, 1))
-            ):
-                total = total + dot_nt(operand, acts[chips + 2 * number + part, :height])
-            grad.append(total)
-        grad = jnp.concatenate(grad, 1)
-        unit_, scale = normal(acts[chips + 6, row * rows : (row + 1) * rows, :].astype(f32))
-        gain = gain_ref[...].reshape(1, width)
-        input_grad[row] = (mixed_grad_ref[row] + normal_pull(grad * gain, unit_, scale)).astype(bf16)
-
-    @pl.loop(ready, max(end, spots[-1] + 1, QUERY_SLOTS[-1] + 1))
+        operands = [jnp.concatenate(keys, 1), jnp.concatenate(values, 1)]
+        result_acc[row * rows : (row + 1) * rows, :] = normed_part(row, operands, 1)
+
+    def last(row):
+        at = slice(row * rows, (row + 1) * rows)
+        grad = result_acc[at, :] + normed_part(row, [columns_of(got_query, row, rows, blocks)], 0)
+        unit_, scale = normal(acts[chips + 6, at, :].astype(f32))
+        pulled = normal_pull(grad * first_gain[...].reshape(1, width), unit_, scale)
+        acts[chips + 7, at, :] = (second_acc[at, :] + pulled).astype(bf16)
+        return pltpu.make_async_copy(acts.at[chips + 7, pl.ds(row * rows, rows)], input_grad.at[row], save.at[row])
+
+    def wait_for(kind):
+        @pl.loop(0, blocks)
+        def _(block):
+            @pl.when(block != me)
+            def _():
+                arrive(kind, block).wait_recv()
+
+    @pl.loop(ready, max(end, ready + max(PAIR_SUM_SLOTS + QUERY_SUM_SLOTS) + 1))
     def _(time):
-        for number, spot in enumerate(spots):
-
-            @pl.when(time == spot)
-            def _():
-                units.step(number + 1)
+        for unit, places in ((pair_sum, PAIR_SUM_SLOTS), (query_sum, QUERY_SUM_SLOTS)):
+            for number, place in enumerate(places):
+
+                @pl.when(time == ready + place)
+                def _():
+                    unit.step(number + 1)
 
         slot(time)
+
+        @pl.when(time == PAIR_DONE)
+        def _():
+            wait_for("pair")
+            for row in range(micro):
+                pair_part(row)
+
+    wait_for("query")
+    saves = [last(row) for row in range(micro)]
+    for copy in saves:
+        copy.start()
 
     @pl.loop(0, blocks)
     def _(block):
         @pl.when(block != me)
         def _():
-            arrive("query", block).wait_recv()
-            arrive("pair", block).wait_recv()
-
-    for row in range(micro):
-        last(row)
-
-    @pl.loop(0, blocks)
-    def _(block):
-        @pl.when(block != me)
-        def _():
             send("grad", block).wait_send()
             send("query", block).wait_send()
             send("pair", block).wait_send()
 
+    theirs = pl.ds(pl.multiple_of((1 - core) * side, 16), side)
     for piece in range(count - GIVE, count):
-        sums.to_core(piece, give.at[piece % GIVE]).wait_send()
+        sums.to_core(piece, give.at[piece % GIVE, theirs]).wait_send()
 
     @pl.loop(0, count)
     def _(piece):
         sums.finish(piece)
 
-    units.finish()
-
-
-def dense_kernel(
-    received, x_ref, up_ref, gain_ref, wo_in, we_in, wc_in,
-    result_ref, mixed_grad_ref, attended_grad_ref, acts_out,
-    wo, we, wc, acts, mixed, result_acc, second_acc, load, store,
-):
-    micro, rows, width = x_ref.shape
-    blocks = received.shape[0]
-    parts = we.shape[0]
-    chips = blocks // 2
-    heads = width // HEAD // chips
-    fetch = [pltpu.make_async_copy(wo_in, wo, load.at[0])]
-    for part in range(parts):
-        cols = pl.ds(part * width, width)
-        fetch.append(pltpu.make_async_copy(we_in.at[:, cols], we.at[part], load.at[1 + 2 * part]))
-        fetch.append(pltpu.make_async_copy(wc_in.at[cols, :], wc.at[part], load.at[2 + 2 * part]))
-    for copy in fetch:
-        copy.start()
-
-    def keep(block):
-        return pltpu.make_async_copy(acts.at[block], acts_out.at[block], store.at[block])
-
-    gain = gain_ref[...].reshape(1, width)
-    low, up, attended, branch = 2 * parts, 2 * parts + 1, 2 * parts + 2, 2 * parts + 3
-    for row in range(micro):
-        at = slice(row * rows, (row + 1) * rows)
-        acts[attended, at, :] = columns_of(received, row, rows, blocks)
-        acts[up, at, :] = up_ref[row]
-    fetch[0].wait()
-    mixed[...] = dot_nn(acts[attended], wo[...])
-    for row in range(micro):
-        at = slice(row * rows, (row + 1) * rows)
-        mixed[at, :] += x_ref[row].astype(f32)
-        unit, _ = normal(mixed[at, :])
-        acts[low, at, :] = (unit * gain).astype(bf16)
-    result_acc[...] = mixed[...]
-    second_acc[...] = jnp.zeros_like(second_acc)
-    for block in (up, attended, low):
-        keep(block).start()
-
-    for part in range(parts):
-        fetch[1 + 2 * part].wait()
-        fetch[2 + 2 * part].wait()
-
-        @pl.loop(0, micro)
-        def _(row):
-            at = pl.ds(pl.multiple_of(row * rows, rows), rows)
-            hidden = dot_nn(acts[low, at, :], we[part])
-            active_grad = dot_nt(acts[up, at, :], wc[part])
-            square = hidden * hidden
-            c = 0.7978845608028654
-            bend = jnp.tanh(hidden * (c + 0.044715 * c * square))
-            gate = 0.5 + 0.5 * bend
-            slope = gate + 0.5 * hidden * (1.0 - bend * bend) * (c + 3.0 * 0.044715 * c * square)
-            active = (hidden * gate).astype(bf16)
-            grad = (active_grad * slope).astype(bf16)
-            acts[part, at, :] = active
-            acts[parts + part, at, :] = grad
-            result_acc[at, :] += dot_nn(active, wc[part])
-            second_acc[at, :] += dot_nt(grad, we[part])
-
-        keep(part).start()
-        keep(parts + part).start()
-
-    for row in range(micro):
-        at = slice(row * rows, (row + 1) * rows)
-        unit, scale = normal(mixed[at, :])
-        grad = acts[up, at, :].astype(f32) + normal_pull(second_acc[at, :] * gain, unit, scale)
-        mixed_grad_ref[row] = grad
-        acts[branch, at, :] = grad.astype(bf16)
-    keep(branch).start()
-    back = dot_nt(acts[branch], wo[...]).astype(bf16)
-    for row in range(micro):
-        at = slice(row * rows, (row + 1) * rows)
-        result_ref[row] = result_acc[at, :].astype(bf16)
-        for chip in range(chips):
-            start = chip * heads * HEAD
-            wide, narrow = pack_heads(
-                [back[at, start + h * HEAD : start + (h + 1) * HEAD] for h in range(heads)]
-            )
-            attended_grad_ref[2 * chip + row, :rows, :] = wide
-            attended_grad_ref[2 * chip + row, rows:, :] = narrow
-    for block in range(2 * parts + 4):
-        keep(block).wait()
+    pair_sum.finish()
+    query_sum.finish()
+    for copy in saves:
+        copy.wait()
 
 
 def final_kernel(
-    final, we_ref, unit_ref, first_gain, second_gain, wq_ref, wkv_ref,
+    final, we_ref, first_gain, second_gain, pair_in, query_in, wq_in, wkv_in,
     first_ref, query_ref, pair_ref, output_ref, second_ref, expand_ref, contract_ref,
-    first_acc, second_acc,
+    first_acc, second_acc, pair_unit, query_unit, wq_ref, wkv_ref, fetch,
 ):
     step = pl.program_id(0)
     width = wq_ref.shape[0]
-    chips = unit_ref.shape[0]
+    chips = pair_in.shape[0]
     heads = width // HEAD // chips
     parts = (pl.num_programs(0) - 4) // 2
 
     def fold(array):
         return sum(array[:, i : i + LANES] for i in range(0, width, LANES))
 
+    def loads():
+        pairs = ((pair_in, pair_unit), (query_in, query_unit), (wq_in, wq_ref), (wkv_in, wkv_ref))
+        return [pltpu.make_async_copy(src, dst, fetch.at[i]) for i, (src, dst) in enumerate(pairs)]
+
     @pl.when(step == 0)
     def _():
+        for copy in loads():
+            copy.start()
         first_acc[...] = jnp.zeros_like(first_acc)
         second_acc[...] = jnp.zeros_like(second_acc)
 
@@ -1302,14 +1369,16 @@
     def _():
         output_ref[...] = final[0].astype(f32)
 
-    def columns(place):
+    def columns(unit, place):
         return jnp.concatenate(
-            [unit_ref[chip][:, place(head) : place(head) + HEAD] for chip in range(chips) for head in range(heads)], 1
+            [unit[chip][:, place(head) : place(head) + HEAD] for chip in range(chips) for head in range(heads)], 1
         ).astype(f32)
 
     @pl.when(step == 2 * parts + 1)
     def _():
-        value = columns(lambda head: heads * LANES + head * HEAD)
+        for copy in loads():
+            copy.wait()
+        value = columns(query_unit, lambda head: head * HEAD)
         query_ref[...] = value
         first_acc[...] += fold(value * wq_ref[...].astype(f32))
 
@@ -1317,7 +1386,7 @@
 
         @pl.when(step == 2 * parts + 2 + side)
         def _():
-            value = columns(lambda head: head * LANES + (HEAD if side == 0 else 0))
+            value = columns(pair_unit, lambda head: head * LANES + (HEAD if side == 0 else 0))
             pair_ref[...] = value
             first_acc[...] += fold(value * wkv_ref[:, side * width : (side + 1) * width].astype(f32))
 
@@ -1350,7 +1419,7 @@
             shape((blocks, packed, LANES), bf16),
             shape((blocks, packed, LANES), bf16),
         ),
-        in_specs=[SMEM, SMEM] + [VMEM] * 5,
+        in_specs=[SMEM, SMEM] + [VMEM] * 3 + [ANY] * 2,
         out_specs=(ANY,) * 5 + (VMEM,),
         scratch_shapes=[
             pltpu.VMEM((blocks, rows, width), bf16),
@@ -1359,9 +1428,12 @@
             pltpu.VMEM(unit, bf16),
             pltpu.VMEM(unit, f32),
             pltpu.VMEM((width, heads * 3 * LANES), bf16),
+            pltpu.VMEM(query_weight.shape, bf16),
+            pltpu.VMEM(pair_weight.shape, bf16),
             pltpu.VMEM((rows, width), bf16),
             pltpu.VMEM(unit, f32),
             pltpu.VMEM((blocks, packed, LANES), bf16),
+            dma((2,)),
             dma,
             dma,
             dma((blocks, 2)),
@@ -1371,101 +1443,77 @@
             dma((blocks, 5)),
         ],
         compiler_params=pltpu.CompilerParams(
-            collective_id=0, has_side_effects=True, vmem_limit_bytes=50 << 20
+            collective_id=0, has_side_effects=True, vmem_limit_bytes=63 << 20
         ),
         name="attention_forward",
     )(lengths, views, inputs, gain, padding, query_weight, pair_weight)
 
 
-def attention_backward(grad, mixed_grad, gain, acts, normed, qa, ka, va, out, query_weight, pair_weight, inputs):
+def attention_backward(
+    first_gain, second_gain, received, inputs, cotangent, normed, qa, ka, va, out,
+    query_weight, pair_weight, output_weight, expand_weight, contract_weight,
+):
     micro, rows, width = inputs.shape
-    blocks, packed, _ = grad.shape
+    blocks, packed, _ = received.shape
     heads, total, _ = qa.shape
     chips = blocks // 2
-    pieces = acts.shape[0] - 3
+    tokens = micro * rows
+    parts = expand_weight.shape[1] // width
+    pieces = 2 * parts + 1
     count = 2 * pieces
-    unit_lanes = (heads + 2) * LANES
     side = width // 2
+    flat = (heads * total, LANES)
     shape = jax.ShapeDtypeStruct
     dma = pltpu.SemaphoreType.DMA
-    unit = pltpu.VMEM((heads, total, LANES), bf16)
     message = pltpu.VMEM((blocks, packed, LANES), bf16)
-    pair = pltpu.VMEM((blocks, heads * rows, LANES), bf16)
     return pl.pallas_call(
         backward_kernel,
         out_shape=(
             shape(inputs.shape, bf16),
+            shape(inputs.shape, bf16),
             shape((pieces, width, width), bf16),
-            shape((chips, width, unit_lanes), bf16),
+            shape((chips, width, heads * LANES), bf16),
+            shape((chips, width, 2 * LANES), bf16),
         ),
-        in_specs=[VMEM] * 3 + [ANY] * 9,
-        out_specs=(VMEM, ANY, ANY),
+        in_specs=[VMEM] * 2 + [ANY] * 13,
+        out_specs=(VMEM, ANY, ANY, ANY, ANY),
         scratch_shapes=[
-            pltpu.VMEM(acts.shape, bf16),
-            unit,
-            unit,
-            unit,
+            pltpu.VMEM((2 * parts + 4, tokens, width), bf16),
+            pltpu.VMEM((2 * parts * width // LANES * width, LANES), bf16),
+            pltpu.VMEM((tokens, width), f32),
+            pltpu.VMEM((tokens, width), f32),
             message,
             message,
-            unit,
-            unit,
+            message,
             pltpu.VMEM((heads, HEAD, total), bf16),
             pltpu.VMEM((heads, HEAD, total), f32),
             pltpu.VMEM((heads, 2 * rows, LANES), f32),
             message,
-            pair,
+            pltpu.VMEM((blocks, heads * rows, LANES), bf16),
             message,
-            pair,
-            pltpu.VMEM((side, unit_lanes), f32),
-            pltpu.VMEM((GIVE, side, side), bf16),
-            dma((acts.shape[0],)),
+            pltpu.VMEM((GIVE, width, side), bf16),
+            dma((2 * parts * width // LANES,)),
+            dma((3 + 2 * micro,)),
             dma((4,)),
             dma((chips + 6 + micro,)),
         ]
         + [dma((blocks,))] * 6
+        + [dma((micro,))]
         + Sums.scratch(count, side, side)
-        + UnitSum.scratch(chips, side, unit_lanes),
+        + UnitSum.scratch(chips, side, heads * LANES)
+        + UnitSum.scratch(chips, side, 2 * LANES),
         compiler_params=pltpu.CompilerParams(
-            collective_id=1, has_side_effects=True, vmem_limit_bytes=62 << 20
+            collective_id=1, has_side_effects=True, vmem_limit_bytes=63 << 20
         ),
-        name="attention_backward",
-    )(grad, mixed_grad, gain, acts, normed, qa, ka, va, out, query_weight, pair_weight, inputs)
-
-
-def dense(received, inputs, cotangent, gain, output_weight, expand_weight, contract_weight):
-    micro, rows, width = inputs.shape
-    tokens = micro * rows
-    parts = expand_weight.shape[1] // width
-    shape = jax.ShapeDtypeStruct
-    dma = pltpu.SemaphoreType.DMA
-    acts = (2 * parts + 4, tokens, width)
-    return pl.pallas_call(
-        dense_kernel,
-        out_shape=(
-            shape((micro, rows, width), bf16),
-            shape((micro, rows, width), f32),
-            shape(received.shape, bf16),
-            shape(acts, bf16),
-        ),
-        in_specs=[VMEM] * 4 + [ANY] * 3,
-        out_specs=(VMEM,) * 3 + (ANY,),
-        scratch_shapes=[
-            pltpu.VMEM((width, width), bf16),
-            pltpu.VMEM((parts, width, width), bf16),
-            pltpu.VMEM((parts, width, width), bf16),
-            pltpu.VMEM(acts, bf16),
-            pltpu.VMEM((tokens, width), f32),
-            pltpu.VMEM((tokens, width), f32),
-            pltpu.VMEM((tokens, width), f32),
-            dma((1 + 2 * parts,)),
-            dma((acts[0],)),
-        ],
-        compiler_params=pltpu.CompilerParams(vmem_limit_bytes=56 << 20),
-        name="dense",
-    )(received, inputs, cotangent, gain, output_weight, expand_weight, contract_weight)
-
-
-def finish(final, unit_final, first_gain, second_gain, query_weight, pair_weight, expand_weight):
+        name="backward",
+    )(
+        first_gain, second_gain, received, inputs, cotangent, normed,
+        qa.reshape(flat), ka.reshape(flat), va.reshape(flat), out,
+        query_weight, pair_weight, output_weight, expand_weight, contract_weight,
+    )
+
+
+def finish(final, pair_final, query_final, first_gain, second_gain, query_weight, pair_weight, expand_weight):
     pieces, width, _ = final.shape
     steps = pieces + 3
     parts = (pieces - 1) // 2
@@ -1478,7 +1526,8 @@
     def clip(p, start, count):
         return jnp.clip(p - start, 0, count - 1)
 
-    fixed = (unit_final, first_gain, second_gain, query_weight, pair_weight)
+    fixed = (first_gain, second_gain)
+    later = (pair_final, query_final, query_weight, pair_weight)
     row = pl.BlockSpec((width,), lambda p: (0,))
     return pl.pallas_call(
         final_kernel,
@@ -1496,7 +1545,8 @@
             pl.BlockSpec((1,) + square, lambda p: (clip(p, 0, pieces), 0, 0)),
             pl.BlockSpec(square, lambda p: (0, clip(p, parts, parts))),
         ]
-        + [whole(array) for array in fixed],
+        + [whole(array) for array in fixed]
+        + [ANY] * 4,
         out_specs=(
             row,
             pl.BlockSpec(square, lambda p: (0, 0)),
@@ -1506,10 +1556,12 @@
             pl.BlockSpec(square, lambda p: (0, clip(p, parts, parts))),
             pl.BlockSpec(square, lambda p: (clip(p, 0, parts), 0)),
         ),
-        scratch_shapes=[pltpu.VMEM((width, LANES), f32), pltpu.VMEM((width, LANES), f32)],
-        compiler_params=pltpu.CompilerParams(vmem_limit_bytes=56 << 20),
+        scratch_shapes=[pltpu.VMEM((width, LANES), f32), pltpu.VMEM((width, LANES), f32)]
+        + [pltpu.VMEM(array.shape, bf16) for array in later]
+        + [pltpu.SemaphoreType.DMA((4,))],
+        compiler_params=pltpu.CompilerParams(vmem_limit_bytes=63 << 20),
         name="finish",
-    )(final, expand_weight, *fixed)
+    )(final, expand_weight, *fixed, *later)
 
 
 def layer_norm(value, gain):
@@ -1822,14 +1874,12 @@
     normed, qa, ka, va, out, received = attention_forward(
         inputs, first_gain, lengths, view_counts, padding, query_weight, key_value_weight, lax.axis_size("blk")
     )
-    result, mixed_grad, attended_grad, acts = dense(
-        received, inputs, cotangent, second_gain, output_weight, expand_weight, contract_weight
-    )
-    input_grad, final, unit_final = attention_backward(
-        attended_grad, mixed_grad, first_gain, acts, normed, qa, ka, va, out, query_weight, key_value_weight, inputs
+    result, input_grad, final, pair_final, query_final = attention_backward(
+        first_gain, second_gain, received, inputs, cotangent, normed, qa, ka, va, out,
+        query_weight, key_value_weight, output_weight, expand_weight, contract_weight,
     )
     first, query, pair, output, second, expand, contract = finish(
-        final, unit_final, first_gain, second_gain, query_weight, key_value_weight, expand_weight
+        final, pair_final, query_final, first_gain, second_gain, query_weight, key_value_weight, expand_weight
     )
     return result, input_grad, first, query, pair, output, second, expand, contract
 

time: 299 us -> 284 us (0.950)
  Pallas kernels: 288 us -> 277 us
  local copies, waits for them, and re-layouts: 7.8 us -> 2.95 us
    pallas_call x1 -> x0, Pallas kernels: 19.7 us -> none  [dense(): pl.pallas_call(dense_kernel, out_shape=(shape((micro, rows, width), bf16)...]
    pallas_call x1, Pallas kernels: 156 us -> 164 us  [attention_backward(): pl.pallas_call(backward_kernel, out_shape=(shape(inputs.shape, bf16), sha...]
    unnamed x19 -> x4, local copies, waits for them, and re-layouts: 7.8 us -> 2.95 us
where the time goes in v3:
time: 284 us; the launch traced here: 281 us
  Pallas kernels  277 us (98%)
  local copies, waits for them, and re-layouts  2.95 us (1%)
    pallas_call x1, Pallas kernels, attention_backward(): pl.pallas_call(backward_kernel, out_shape=(shape(inputs.shape, bf16), sha...  164 us
    pallas_call x1, Pallas kernels, attention_forward(): pl.pallas_call(forward_kernel, out_shape=(shape((blocks // 2, 2 * rows, w...  90.9 us
    pallas_call x1, Pallas kernels, finish(): pl.pallas_call(final_kernel, grid=(steps,), out_shape=(shape((width,), f3...  22.1 us

profile of v3, /device:TPU:0, one launch (start us, length us, event | category | flops | bytes accessed | tf_op | source)
XLA Modules:
  0.0 280.6 jit_solution(227221297091136639)
XLA Ops:
  0.6 90.9 %attention_forward.1 = (bf16[4,512,768]{2,1,0:T(8,128)(2,1)}, bf16[3,2048,128]{2,1,0:T(8,128)(2,1)}, bf16[3,2048,128]{2,1,0:T(8,128)(2,1)}, bf16[3,2048,128]{2,1...) custom-call(s32[2,4]{1,0:T(2,128)} %lengths.1, s32[2,4]{1,0:T(2,128)} %views.1, ...), custom_call_target="tpu_custom_call" | custom-call | tf_op jit(solution)/shard_map/attention_forward/pallas_call | solution.py:1412
  91.5 163.7 %backward.1 = (bf16[2,256,768]{2,1,0:T(8,128)(2,1)}, bf16[2,256,768]{2,1,0:T(8,128)(2,1)}, bf16[9,768,768]{2,1,0:T(8,128)(2,1)}, bf16[4,768,384]{2,1,0:T(8,128)(2,1)}, bf16[4,768,256]{2,1,0:T(8,128)(2,1)}) custom-call(f32[768]{0:T(1024)} %first_gain.3, f32[768]{0:T(1024)} %second_gain.3, bf16[8,384,128]{2,1,0:T(8,128)(2,1)} %get-tuple-element.27.received_in, ...), custom_call_target="tpu_custom_call" | custom-call | tf_op jit(solution)/shard_map/backward/pallas_call | solution.py:1469
  255.2 0.0 copy-start
  255.2 22.1 %finish.1 = (f32[768]{0:T(1024)}, f32[768,768]{1,0:T(8,128)}, f32[768,1536]{1,0:T(8,128)}, f32[768,768]{1,0:T(8,128)}, f32[768]{0:T(1024)}, /*index=5*/f32[768,3072]{1,0:T(8,128)}, f32[3072,768]{1,0:T(8,128)}) custom-call(bf16[9,768,768]{2,1,0:T(8,128)(2,1)} %get-tuple-element.35.final, bf16[768,3072]{1,0:T(8,128)(2,1)} %we_ref.1, f32[768]{0:T(1024)} %first_gain.3, ...), custom_call_target="tpu_custom_call" | custom-call | tf_op jit(solution)/shard_map/finish/pallas_call | solution.py:1532
  277.4 2.1 copy.23
  279.5 0.0 copy-done
  279.5 0.9 copy.24
Async XLA Ops:
  255.2 24.2 %copy-start = (bf16[2,256,768]{2,1,0:T(8,128)(2,1)S(1)}, bf16[2,256,768]{2,1,0:T(8,128)(2,1)}, u32[]{:S(2)}) copy-start(bf16[2,256,768]{2,1,0:T(8,128)(2,1)} %get-tuple-element.55) | copy-start | bytes 2359300
